TPU v7x, 256 devices: a whole 4x4x8 slice. The times are simulated.
256 devices in a mesh: gx: 4 (over z_hi), gy: 4 (over x), gz: 16 (over z_lo, y, core).
Axes of the slice: x: 4, y: 4, z: 8 (z_hi: 4, z_lo: 2; z = z_hi * 2 + z_lo), core: 2. Of those that a mesh axis runs over, the one named last changes fastest.
Arguments:
- volume_features: bfloat16 [64, 128, 256, 64], P('gx', 'gy', 'gz'), may hold values from -6 to 6
- fine_weight: bfloat16 [3, 3, 3, 64, 64], replicated, may hold values from -0.21875 to 0.21875
- fine_bias: float32 [64], replicated, may hold values from -1.5 to 1.5
- middle_weight: bfloat16 [3, 3, 3, 64, 128], replicated, may hold values from -0.21875 to 0.21875
- middle_bias: float32 [128], replicated, may hold values from -1.5 to 1.5
- bottom_weight: bfloat16 [3, 3, 3, 128, 256], replicated, may hold values from -0.15625 to 0.15625
- bottom_bias: float32 [256], replicated, may hold values from -1.5 to 1.5
- rise_middle_weight: bfloat16 [3, 3, 3, 384, 128], replicated, may hold values from -0.078125 to 0.078125
- rise_middle_bias: float32 [128], replicated, may hold values from -1.5 to 1.5
- rise_fine_weight: bfloat16 [3, 3, 3, 192, 64], replicated, may hold values from -0.125 to 0.125
- rise_fine_bias: float32 [64], replicated, may hold values from -1.5 to 1.5
Outputs:
- decoded: bfloat16 [64, 128, 256, 64], P('gx', 'gy', 'gz')
All inputs are finite; a program needn't handle non-finite values.
Results may differ from a plain program's by a relative error of at most 0.012.
Values may be sent and summed in bfloat16 or wider, within the bound.
A program may use at most 128 MiB of HBM per device.

v0:
```python
import functools

import jax
import jax.numpy as jnp
from jax import lax
from jax.experimental import pallas as pl
from jax.experimental.pallas import tpu as pltpu
from jax.sharding import PartitionSpec as P

BF = jnp.bfloat16
F32 = jnp.float32
MESH = pl.DeviceIdType.MESH

NXF, NZF, ROWS = 16, 16, 16
NXM, NZM = 8, 8
TF, TM = 336, 112
LEVELS = 6


def dot(a, b):
    return jnp.dot(a, b, preferred_element_type=F32)


def cells(ref, *index):
    value = ref[index]
    return value.reshape(-1, value.shape[-1])


def kernel(
    sizes,
    vol, wf_hbm, wm_hbm, wb_hbm, wrm_hbm, wrf_hbm, bias_ref,
    out_hbm,
    r_in, h_in, s_fine, y_in, yr_in,
    r_enc, h_enc, y_enc, yr_enc,
    r_pool, h_pool, s_pool, y_pool, yr_pool,
    r_mid, hu_mid, hd_mid, s_mid, y_mid, yr_mid,
    r_low, s_low, y_low, yr_low, pair_tmp,
    low_lanes, bottom_tmp, s_up, up_lanes,
    r_dec, hu_dec, hd_dec, s_dec, y_dec, yr_dec,
    wf_raw, wrf_raw, wrm_raw,
    w_fine, w_skip, w_mid, w_bottom, w_rm_skip, w_rm_up, w_rf_up,
    skip, out_v,
    send_sem, recv_sem, local_sem,
):
    spots = {axis: lax.axis_index(axis) for axis in ("gx", "gy", "gz")}

    def near(axis, step):
        count = sizes[axis]
        return lax.rem(spots[axis] + (step + count), count)

    def at_low(axis):
        return spots[axis] == 0

    def at_high(axis):
        return spots[axis] == sizes[axis] - 1

    def message(number, src, dst, axis, step):
        return pltpu.make_async_remote_copy(
            src_ref=src, dst_ref=dst, send_sem=send_sem.at[number], recv_sem=recv_sem.at[number],
            device_id={axis: near(axis, step)}, device_id_type=MESH,
        )

    sent = []

    def start(copies):
        for copy in copies:
            copy.start()
        sent.extend(copies)
        return copies

    def arrived(copies):
        for copy in copies:
            copy.wait_recv()

    loads = {}

    def load(name, src, dst):
        copy = pltpu.make_async_copy(src, dst, local_sem.at[len(loads)])
        copy.start()
        loads[name] = copy

    load("vol0", vol.at[:, :, 0], r_in.at[1:NXF + 1, 0:8, 1])
    load("vol1", vol.at[:, :, 1], r_in.at[1:NXF + 1, 1:9, 0])
    load("wf", wf_hbm, wf_raw)
    load("wrf", wrf_hbm, wrf_raw)
    for dz in range(2):
        lanes = pl.ds(dz * 128, 128)
        for q, slot in ((1, 0), (2, 2), (0, 3)):
            load(("wm", dz, q), wm_hbm.at[:, q], w_mid.at[:, dz:dz + 3, slot, :, lanes])
    for q, slot in ((1, 0), (2, 1), (0, 2)):
        load(("wb", q), wb_hbm.at[:, q], w_bottom.at[:, :, slot])
    for dz in range(2):
        lanes = pl.ds(dz * 128, 128)
        for q, slot in ((1, 0), (2, 1), (0, 2)):
            load(("wrm", dz, q), wrm_hbm.at[:, q, :, 0:128, :], w_rm_skip.at[:, dz:dz + 3, slot, :, lanes])
    load("wrm_raw", wrm_hbm.at[:, :, :, 128:384, :], wrm_raw)

    barrier = pltpu.get_barrier_semaphore()
    for axis in ("gx", "gy", "gz"):
        for step in (-1, 1):
            pl.semaphore_signal(barrier, inc=1, device_id={axis: near(axis, step)}, device_id_type=MESH)
    pl.semaphore_wait(barrier, 6)

    def start_z(base, ref, nx, nz):
        own = pl.ds(1, nx)
        return start([
            message(base, ref.at[own, 0, 1], ref.at[own, nz // 2, 1], "gz", -1),
            message(base + 1, ref.at[own, nz // 2, 0], ref.at[own, 0, 0], "gz", 1),
        ])

    def wait_z(copies, ref, s, nx, nz):
        arrived(copies)
        own = pl.ds(1, nx)

        @pl.when(at_low("gz"))
        def _():
            ref[own, 0, 0] = jnp.zeros((nx, ROWS, 128), BF)

        @pl.when(at_high("gz"))
        def _():
            ref[own, nz // 2, 1] = jnp.zeros((nx, ROWS, 128), BF)

        s[own, 0, 0, 8:24] = ref[own, 0, 0].astype(F32)
        s[own, nz // 2, 1, 8:24] = ref[own, nz // 2, 1].astype(F32)

    def start_x(base, ref, nx):
        return start([
            message(base + 2, ref.at[1], ref.at[nx + 1], "gx", -1),
            message(base + 3, ref.at[nx], ref.at[0], "gx", 1),
        ])

    def wait_x(copies, ref, s, nx):
        arrived(copies)
        for plane, edge in ((0, at_low("gx")), (nx + 1, at_high("gx"))):
            @pl.when(edge)
            def _():
                ref[plane] = jnp.zeros(ref.shape[1:], BF)

            s[plane, :, :, 8:24] = ref[plane].astype(F32)

    def start_y(base, s, ys, yr):
        count = ys.shape[1]
        rows = s.reshape(s.shape[0] * s.shape[1] * s.shape[2] * 32, 128)
        ys[0] = rows[pl.ds(8, count, stride=32), :].astype(BF)
        ys[1] = rows[pl.ds(23, count, stride=32), :].astype(BF)
        return start([
            message(base + 4, ys.at[0], yr.at[1], "gy", -1),
            message(base + 5, ys.at[1], yr.at[0], "gy", 1),
        ])

    def wait_y(copies, s, yr):
        arrived(copies)
        count = yr.shape[1]
        rows = s.reshape(s.shape[0] * s.shape[1] * s.shape[2] * 32, 128)
        low = jnp.where(at_low("gy"), 0.0, yr[0].astype(F32))
        high = jnp.where(at_high("gy"), 0.0, yr[1].astype(F32))
        rows[pl.ds(7, count, stride=32), :] = low
        rows[pl.ds(24, count, stride=32), :] = high

    def beside(s, dst, planes):
        lane = lax.broadcasted_iota(jnp.int32, dst.shape[1:], 3)

        def plane(x, carry):
            dst[x] = jnp.where(lane < 64, s[x, :, :, 9:25], s[x, :, :, 7:23]).astype(BF)
            return carry

        lax.fori_loop(0, planes, plane, 0)

    def beside_both(s, up, down, planes):
        def plane(x, carry):
            up[x] = s[x, :, :, 9:25].astype(BF)
            down[x] = s[x, :, :, 7:23].astype(BF)
            return carry

        lax.fori_loop(0, planes, plane, 0)

    def spread(raw, first, dst):
        dst[...] = jnp.zeros(dst.shape, BF)

        def one(p, carry):
            for r in range(3):
                taps = [raw[p, q, r, first:first + 64, :] for q in range(3)]
                none = jnp.zeros_like(taps[0])
                pairs = ((taps[1], taps[0]), (taps[2], taps[1]), (none, taps[2]), (taps[0], none))
                for slot, pair in enumerate(pairs):
                    block = jnp.concatenate(pair, axis=1)
                    for dz in range(2):
                        dst[p, r + dz, slot, :, dz * 128:(dz + 1) * 128] = block
            return carry

        lax.fori_loop(0, 3, one, 0)

    def fine_window(ref, side, x, count):
        parts = []
        for p in range(3):
            for zo in range(4):
                index = (pl.ds(x + p, count), pl.ds(zo // 2, 8), zo % 2)
                parts += [cells(ref, *index), cells(side, *index)]
        return jnp.concatenate(parts, axis=1)

    loads["vol0"].wait()
    loads["vol1"].wait()
    going = start_z(0, r_in, NXF, NZF)

    def widen(x, carry):
        s_fine[x, 0:8, 1, 8:24] = r_in[x, 0:8, 1].astype(F32)
        s_fine[x, 1:9, 0, 8:24] = r_in[x, 1:9, 0].astype(F32)
        return carry

    lax.fori_loop(1, NXF + 1, widen, 0)
    loads["wf"].wait()
    spread(wf_raw, 0, w_fine)
    wait_z(going, r_in, s_fine, NXF, NZF)
    going = start_x(0, r_in, NXF)
    w_mid[:, :, 1] = jnp.zeros((3, 4, 64, 256), BF)
    w_mid[:, 3, :, :, 0:128] = jnp.zeros((3, 4, 64, 128), BF)
    w_mid[:, 0, :, :, 128:256] = jnp.zeros((3, 4, 64, 128), BF)
    w_rm_skip[:, 3, :, :, 0:128] = jnp.zeros((3, 3, 128, 128), BF)
    w_rm_skip[:, 0, :, :, 128:256] = jnp.zeros((3, 3, 128, 128), BF)
    loads["wrf"].wait()
    spread(wrf_raw, 0, w_skip)
    wait_x(going, r_in, s_fine, NXF)
    going = start_y(0, s_fine, y_in, yr_in)
    wait_y(going, s_fine, yr_in)
    beside(s_fine, h_in, NXF + 2)

    w_fine_all = w_fine.reshape(3072, 256)

    def fine(pair, carry):
        x = 2 * pair
        result = dot(fine_window(r_in, h_in, x, 2), w_fine_all[...])
        result = jnp.maximum(result + bias_ref[0:1, :], 0.0).reshape(2, 8, ROWS, 256)
        for dz, (index, half) in enumerate((((pl.ds(0, 8), 1), 0), ((pl.ds(1, 8), 0), 1))):
            value = result[..., half * 128:(half + 1) * 128]
            r_enc[(pl.ds(x + 1, 2),) + index] = value.astype(BF)
            s_fine[(pl.ds(x + 1, 2),) + index + (pl.ds(8, 16),)] = value
        most = jnp.max(result, axis=0)
        most = jnp.maximum(most[..., 0:128], most[..., 128:256]).reshape(128, 128)
        most = jnp.maximum(most, pltpu.roll(most, 64, 1)).reshape(4, 2, ROWS, 128)
        r_pool[pair + 1, 0:4, 1] = most[:, 0].astype(BF)
        s_pool[pair + 1, 0:4, 1, 8:24] = most[:, 0]
        r_pool[pair + 1, 1:5, 0] = most[:, 1].astype(BF)
        s_pool[pair + 1, 1:5, 0, 8:24] = most[:, 1]
        return carry

    lax.fori_loop(0, 8, fine, 0)

    going = start_z(6, r_pool, NXM, NZM)
    skipping = start_z(12, r_enc, NXF, NZF)
    loads["wrm_raw"].wait()

    def sums(parts):
        return (parts[0], parts[1] + parts[2], parts[0] + parts[1], parts[2])

    def rise_mid(chunk, carry):
        rows = pl.ds(pl.multiple_of(chunk * 16, 16), 16)
        for q, slot in ((1, 0), (2, 1), (0, 2)):
            by_r = [sums([wrm_raw[p, q, r, rows, :].astype(F32) for p in range(3)]) for r in range(3)]
            for x_sum in range(4):
                z_sums = sums([by_r[r][x_sum] for r in range(3)])
                for z_sum, (zt, dz) in enumerate(((0, 0), (1, 0), (1, 1), (2, 1))):
                    w_rm_up[x_sum, zt, slot, rows, dz * 128:(dz + 1) * 128] = z_sums[z_sum].astype(BF)
        return carry

    w_rm_up[:, 0, :, :, 128:256] = jnp.zeros((4, 3, 256, 128), BF)
    w_rm_up[:, 2, :, :, 0:128] = jnp.zeros((4, 3, 256, 128), BF)
    lax.fori_loop(0, 16, rise_mid, 0)

    wait_z(going, r_pool, s_pool, NXM, NZM)
    going = start_x(6, r_pool, NXM)
    wait_z(skipping, r_enc, s_fine, NXF, NZF)
    skipping = start_x(12, r_enc, NXF)

    def rise_fine(chunk, carry):
        src = pl.ds(pl.multiple_of(64 + chunk * 16, 16), 16)
        rows = pl.ds(pl.multiple_of(chunk * 16, 16), 16)
        by_q = []
        for q in range(3):
            by_r = [sums([wrf_raw[p, q, r, src, :].astype(F32) for p in range(3)]) for r in range(3)]
            by_q.append([sums([by_r[r][x_sum] for r in range(3)]) for x_sum in range(4)])
        none = jnp.zeros((16, 64), F32)
        for x_sum in range(4):
            for z_sum, (zt, dz) in enumerate(((0, 0), (1, 0), (1, 1), (2, 1))):
                taps = [by_q[q][x_sum][z_sum] for q in range(3)]
                pairs = ((taps[1] + taps[2], taps[0] + taps[1]), (none, taps[2]), (taps[0], none))
                for slot, pair in enumerate(pairs):
                    block = jnp.concatenate(pair, axis=1).astype(BF)
                    w_rf_up[x_sum, zt, slot, rows, dz * 128:(dz + 1) * 128] = block
        return carry

    w_rf_up[:, 0, :, :, 128:256] = jnp.zeros((4, 3, 128, 128), BF)
    w_rf_up[:, 2, :, :, 0:128] = jnp.zeros((4, 3, 128, 128), BF)
    lax.fori_loop(0, 8, rise_fine, 0)

    wait_x(going, r_pool, s_pool, NXM)
    going = start_y(6, s_pool, y_pool, yr_pool)
    wait_x(skipping, r_enc, s_fine, NXF)
    skipping = start_y(12, s_fine, y_enc, yr_enc)
    for dz in range(2):
        for q in range(3):
            loads[("wm", dz, q)].wait()
    wait_y(going, s_pool, yr_pool)
    beside(s_pool, h_pool, NXM + 2)

    parts = []
    for p in range(3):
        for zo in range(4):
            index = (pl.ds(p, 8), pl.ds(zo // 2, 4), zo % 2)
            parts += [cells(r_pool, *index), cells(h_pool, *index)]
    result = dot(jnp.concatenate(parts, axis=1), w_mid.reshape(3072, 256)[...])
    result = jnp.maximum(result + bias_ref[1:2, :], 0.0).reshape(4, 2, 4, ROWS, 256)
    for dz, index in enumerate(((pl.ds(0, 4), 1), (pl.ds(1, 4), 0))):
        value = result[..., dz * 128:(dz + 1) * 128]
        for dx in range(2):
            place = (pl.ds(0, 4), 1) if dx == 0 else (pl.ds(1, 4), 0)
            r_mid[place + index] = value[:, dx].astype(BF)
            s_mid[place + index + (pl.ds(8, 16),)] = value[:, dx]
    most = jnp.maximum(result[:, 0], result[:, 1])
    pair_tmp[...] = jnp.maximum(most[..., 0:128], most[..., 128:256]).reshape(256, 128)
    low = jnp.maximum(pair_tmp[pl.ds(0, 128, stride=2), :], pair_tmp[pl.ds(1, 128, stride=2), :])
    r_low[2:6, 1:3] = low.astype(BF).reshape(4, 2, ROWS, 128)

    base = 18
    going = start([
        message(base, r_low.at[2:6, 1], r_low.at[2:6, 3], "gz", -1),
        message(base + 1, r_low.at[2:6, 2], r_low.at[2:6, 0], "gz", 1),
    ])
    r_mid_planes = r_mid.reshape(10, 5, 2, ROWS, 128)
    s_mid_planes = s_mid.reshape(12, 5, 2, 32, 128)
    middle = start_z(24, r_mid_planes, NXM, NZM)

    wait_y(skipping, s_fine, yr_enc)
    beside(s_fine, h_enc, NXF + 2)
    w_skip_all = w_skip.reshape(3072, 256)

    def skip_part(pair, carry):
        x = 2 * pair
        result = dot(fine_window(r_enc, h_enc, x, 2), w_skip_all[...]) + bias_ref[4:5, :]
        skip[pl.ds(x, 2)] = result.reshape(2, 128, 256)
        return carry

    arrived(going)

    @pl.when(at_low("gz"))
    def _():
        r_low[2:6, 0] = jnp.zeros((4, ROWS, 128), BF)

    @pl.when(at_high("gz"))
    def _():
        r_low[2:6, 3] = jnp.zeros((4, ROWS, 128), BF)

    going = start([
        message(base + 2, r_low.at[2:4], r_low.at[6:8], "gx", -1),
        message(base + 3, r_low.at[4:6], r_low.at[0:2], "gx", 1),
    ])
    wait_z(middle, r_mid_planes, s_mid_planes, NXM, NZM)
    middle = start_x(24, r_mid_planes, NXM)
    lax.fori_loop(0, 3, skip_part, 0)
    arrived(going)

    @pl.when(at_low("gx"))
    def _():
        r_low[0:2] = jnp.zeros((2, 4, ROWS, 128), BF)

    @pl.when(at_high("gx"))
    def _():
        r_low[6:8] = jnp.zeros((2, 4, ROWS, 128), BF)

    low = r_low[...].astype(F32).reshape(8, 4, 2, 8, 128).reshape(8, 8, 8, 128)
    s_low[:, :, 8:16] = low
    s_low[:, :, 0:8] = jnp.zeros_like(low)
    s_low[:, :, 16:24] = jnp.zeros_like(low)
    rows = s_low.reshape(2048, 128)
    for number, row in enumerate((8, 9, 14, 15)):
        y_low[number // 2, pl.ds((number % 2) * 64, 64), :] = rows[pl.ds(row, 64, stride=32), :].astype(BF)
    going = start([
        message(base + 4, y_low.at[0], yr_low.at[1], "gy", -1),
        message(base + 5, y_low.at[1], yr_low.at[0], "gy", 1),
    ])
    wait_x(middle, r_mid_planes, s_mid_planes, NXM)
    middle = start_y(24, s_mid_planes, y_mid, yr_mid)
    for q in range(3):
        loads[("wb", q)].wait()
    lax.fori_loop(3, 5, skip_part, 0)
    arrived(going)
    for number, row in enumerate((6, 7, 16, 17)):
        edge = at_low("gy") if number < 2 else at_high("gy")
        value = yr_low[number // 2, pl.ds((number % 2) * 64, 64), :].astype(F32)
        rows[pl.ds(row, 64, stride=32), :] = jnp.where(edge, 0.0, value)

    def low_plane(x, carry):
        for slot, first in enumerate((4, 5, 3)):
            low_lanes[x, :, :, slot * 128:(slot + 1) * 128] = s_low[x, :, first:first + 16].astype(BF)
        return carry

    lax.fori_loop(0, 8, low_plane, 0)
    parts = [cells(low_lanes, pl.ds(p, 6), pl.ds(r, 6)) for p in range(3) for r in range(3)]
    result = dot(jnp.concatenate(parts, axis=1), w_bottom.reshape(3456, 256)[...])
    result = jnp.maximum(result + bias_ref[2:3, :], 0.0).reshape(6, 6, ROWS, 256)
    index = lax.broadcasted_iota(jnp.int32, (6, 6, ROWS, 256), 0)
    zindex = lax.broadcasted_iota(jnp.int32, (6, 6, ROWS, 256), 1)
    yindex = lax.broadcasted_iota(jnp.int32, (6, 6, ROWS, 256), 2)
    outside = False
    for where, first, last, axis in ((index, 0, 5, "gx"), (zindex, 0, 5, "gz"), (yindex, 3, 12, "gy")):
        outside = outside | ((where == first) & at_low(axis)) | ((where == last) & at_high(axis))
    result = jnp.where(outside, 0.0, result).reshape(576, 256)
    for half in range(2):
        bottom_tmp[half] = result[:, half * 128:(half + 1) * 128]

    for half in range(2):
        doubled = s_up.at[half].reshape(36 * 32, 128)
        for step in range(10):
            value = bottom_tmp.at[half][pl.ds(3 + step, 36, stride=16), :]
            doubled[pl.ds(6 + 2 * step, 36, stride=32), :] = value
            doubled[pl.ds(7 + 2 * step, 36, stride=32), :] = value
    for slot, first in enumerate((8, 9, 7)):
        for half in range(2):
            lanes = slice(slot * 256 + half * 128, slot * 256 + half * 128 + 128)
            up_lanes[:, :, :, lanes] = s_up[half, :, first:first + 16].astype(BF).reshape(6, 6, ROWS, 128)

    wait_y(middle, s_mid_planes, yr_mid)
    beside_both(s_mid_planes, hu_mid.reshape(10, 5, 2, ROWS, 128), hd_mid.reshape(10, 5, 2, ROWS, 128), NXM + 2)
    for dz in range(2):
        for q in range(3):
            loads[("wrm", dz, q)].wait()

    for dx in range(2):
        parts = []
        for p in range(3):
            for zo in range(4):
                index = (pl.ds((dx + p) // 2, 4), (dx + p) % 2, pl.ds(zo // 2, 4), zo % 2)
                parts += [cells(ref, *index) for ref in (r_mid, hu_mid, hd_mid)]
        result = dot(jnp.concatenate(parts, axis=1), w_rm_skip.reshape(4608, 256)[...])
        parts = []
        for xt in range(2):
            for zt in range(3):
                parts.append(cells(up_lanes, pl.ds(xt + dx, 4), pl.ds(zt, 4)))
        weight = w_rm_up.reshape(2, 4608, 256)[dx]
        result = result + dot(jnp.concatenate(parts, axis=1), weight)
        result = jnp.maximum(result + bias_ref[3:4, :], 0.0).reshape(4, 4, ROWS, 256)
        for dz, index in enumerate(((pl.ds(0, 4), 1), (pl.ds(1, 4), 0))):
            place = (pl.ds(0, 4), 1) if dx == 0 else (pl.ds(1, 4), 0)
            value = result[..., dz * 128:(dz + 1) * 128]
            r_dec[place + index] = value.astype(BF)
            s_dec[place + index + (pl.ds(8, 16),)] = value

    r_dec_planes = r_dec.reshape(10, 5, 2, ROWS, 128)
    s_dec_planes = s_dec.reshape(12, 5, 2, 32, 128)
    going = start_z(30, r_dec_planes, NXM, NZM)
    lax.fori_loop(5, 6, skip_part, 0)
    wait_z(going, r_dec_planes, s_dec_planes, NXM, NZM)
    going = start_x(30, r_dec_planes, NXM)
    lax.fori_loop(6, 7, skip_part, 0)
    wait_x(going, r_dec_planes, s_dec_planes, NXM)
    going = start_y(30, s_dec_planes, y_dec, yr_dec)
    lax.fori_loop(7, 8, skip_part, 0)
    wait_y(going, s_dec_planes, yr_dec)
    beside_both(s_dec_planes, hu_dec.reshape(10, 5, 2, ROWS, 128), hd_dec.reshape(10, 5, 2, ROWS, 128), NXM + 2)

    flat = [ref.reshape(10, 10, ROWS, 128) for ref in (r_dec, hu_dec, hd_dec)]
    for dx in range(2):
        weight = w_rf_up.reshape(2, 2304, 256)

        def last(step, carry):
            x = 2 * step
            parts = []
            for xt in range(2):
                for zt in range(3):
                    parts += [cells(ref, pl.ds(x + xt + dx, 2), pl.ds(zt, 8)) for ref in flat]
            result = dot(jnp.concatenate(parts, axis=1), weight[dx]).reshape(2, 128, 256)
            for i in range(2):
                spot = 4 * step + 2 * i + dx
                out_v[spot] = (result[i] + skip[spot]).astype(BF).reshape(8, ROWS, 256)
            return carry

        lax.fori_loop(0, 4, last, 0)

    copy = pltpu.make_async_copy(out_v, out_hbm, local_sem.at[len(loads)])
    copy.start()
    for message_sent in sent:
        message_sent.wait_send()
    copy.wait()


def scratch():
    vmem = pltpu.VMEM
    fine = (NXF + 2, 9, 2, ROWS, 128)
    pool = (NXM + 2, 5, 2, ROWS, 128)
    mid = (5, 2, 5, 2, ROWS, 128)
    mid_s = (6, 2, 5, 2, 32, 128)
    return [
        vmem(fine, BF), vmem(fine, BF), vmem((NXF + 3, 9, 2, 32, 128), F32), vmem((2, TF, 128), BF), vmem((2, TF, 128), BF),
        vmem(fine, BF), vmem(fine, BF), vmem((2, TF, 128), BF), vmem((2, TF, 128), BF),
        vmem(pool, BF), vmem(pool, BF), vmem((NXM + 4, 5, 2, 32, 128), F32), vmem((2, TM, 128), BF), vmem((2, TM, 128), BF),
        vmem(mid, BF), vmem(mid, BF), vmem(mid, BF), vmem(mid_s, F32), vmem((2, TM, 128), BF), vmem((2, TM, 128), BF),
        vmem((8, 4, ROWS, 128), BF), vmem((8, 8, 32, 128), F32), vmem((2, 128, 128), BF), vmem((2, 128, 128), BF),
        vmem((256, 128), F32),
        vmem((8, 8, ROWS, 384), BF), vmem((2, 576, 128), F32), vmem((2, 36, 32, 128), F32), vmem((6, 6, ROWS, 768), BF),
        vmem(mid, BF), vmem(mid, BF), vmem(mid, BF), vmem(mid_s, F32), vmem((2, TM, 128), BF), vmem((2, TM, 128), BF),
        vmem((3, 3, 3, 64, 64), BF), vmem((3, 3, 3, 192, 64), BF), vmem((3, 3, 3, 256, 128), BF),
        vmem((3, 4, 4, 64, 256), BF), vmem((3, 4, 4, 64, 256), BF), vmem((3, 4, 4, 64, 256), BF),
        vmem((3, 3, 3, 128, 256), BF), vmem((3, 4, 3, 128, 256), BF), vmem((4, 3, 3, 256, 256), BF),
        vmem((4, 3, 3, 128, 256), BF),
        vmem((NXF, 128, 256), F32), vmem((NXF, 8, ROWS, 256), BF),
        pltpu.SemaphoreType.DMA((6 * LEVELS,)), pltpu.SemaphoreType.DMA((6 * LEVELS,)), pltpu.SemaphoreType.DMA((32,)),
    ]


def on_device(sizes, volume, wf, bf, wm, bm, wb, bb, wrm, brm, wrf, brf):
    block = volume.reshape(NXF, ROWS, 2, 8, 2, 64).transpose(0, 3, 4, 1, 2, 5).reshape(NXF, 8, 2, ROWS, 128)
    bias = jnp.stack([jnp.tile(bf, 4), jnp.tile(bm, 2), bb, jnp.tile(brm, 2), jnp.tile(brf, 4)])
    hbm = pl.BlockSpec(memory_space=pl.ANY)
    result = pl.pallas_call(
        functools.partial(kernel, sizes),
        out_shape=jax.ShapeDtypeStruct((NXF, 8, ROWS, 256), BF),
        in_specs=[hbm] * 6 + [pl.BlockSpec(memory_space=pltpu.VMEM)],
        out_specs=hbm,
        scratch_shapes=scratch(),
        compiler_params=pltpu.CompilerParams(
            collective_id=0, has_side_effects=True, vmem_limit_bytes=60 * 2**20
        ),
    )(block, wf, wm, wb, wrm, wrf, bias)
    return result.reshape(NXF, 8, ROWS, 2, 2, 64).transpose(0, 2, 4, 1, 3, 5).reshape(NXF, 32, NZF, 64)


def solution(mesh):
    return jax.shard_map(
        functools.partial(on_device, dict(mesh.shape)),
        mesh=mesh,
        in_specs=(P("gx", "gy", "gz", None),) + (P(),) * 10,
        out_specs=P("gx", "gy", "gz", None),
        check_vma=False,
    )
```

profile of v0, /device:TPU:2, one launch (start us, length us, event | category | flops | bytes accessed | tf_op | source)
XLA Modules:
  0.0 89.2 jit_solution(11286078277234816842)
XLA Ops:
  0.0 4.1 %copy.16 = bf16[16,16,2,8,2,64]{5,2,1,4,3,0:T(2,128)(2,1)S(1)} copy(bf16[16,16,2,8,2,64]{5,4,3,2,1,0:T(2,128)(2,1)} %bitcast.13) | data formatting | bytes 2097152 | tf_op jit(solution)/shard_map/reshape | solution.py:510
  4.1 0.0 copy-start
  4.1 0.0 copy-start.2
  4.1 0.0 copy-start.3
  4.1 0.0 copy-start.4
  4.1 0.0 copy-start.5
  4.1 0.0 copy-start.1
  4.1 1.8 %reshape.17.vol = bf16[16,8,2,16,128]{4,3,2,1,0:T(8,128)(2,1)} reshape(bf16[16,8,2,16,2,64]{5,4,3,2,1,0:T(2,128)(2,1)S(1)} %bitcast.12) | data formatting | bytes 2097152 | tf_op jit(solution)/shard_map/reshape | solution.py:510
  5.9 0.0 copy-done
  5.9 1.6 %copy.13.wrf_hbm = bf16[3,3,3,192,64]{4,3,2,1,0:T(8,128)(2,1)} copy(bf16[3,3,3,192,64]{3,4,2,1,0:T(8,128)(2,1)S(1)} %copy-done) | data formatting | bytes 1327104 | tf_op args[9]
  7.5 0.0 copy-done.2
  7.5 0.1 stack_tile.12
  7.6 0.0 copy-done.3
  7.6 0.1 stack_tile.15
  7.7 0.0 copy-done.4
  7.7 0.0 copy-done.5
  7.7 0.0 copy-done.1
  7.7 0.6 stack.7.bias_ref
  8.3 73.8 %shard_map.109 = bf16[16,8,16,256]{3,2,1,0:T(8,128)(2,1)} custom-call(bf16[16,8,2,16,128]{4,3,2,1,0:T(8,128)(2,1)} %reshape.17.vol, bf16[3,3,3,64,64]{4,3,2,1,0:T(8,128)(2,1)} %wf_hbm.1, bf16[3,3,3,64,128]{4,3,2,1,0:T(8,128)(2,1)} %wm_hbm.1, bf16[3,3,3,128,256]{4,3,2,1,0:T(8,128)(2,1)} %wb_hbm.1, bf16[3,3,3,384,128]{4,3,2,1,0:T(8,128)(2,1)} %wrm_hbm.1, ...), custom_call_target="tpu_custom_call" | custom-call | tf_op jit(solution)/shard_map/pallas_call | solution.py:513
  82.1 4.0 %reshape.18 = bf16[16,8,16,2,2,64]{5,4,3,2,1,0:T(2,128)(2,1)S(1)} reshape(bf16[16,8,16,256]{3,2,1,0:T(8,128)(2,1)} %shard_map.109) | data formatting | bytes 2097152 | tf_op jit(solution)/shard_map/reshape | solution.py:523
  86.1 3.1 %copy.14 = bf16[16,16,2,8,2,64]{5,4,3,2,1,0:T(2,128)(2,1)} copy(bf16[16,16,2,8,2,64]{5,2,4,1,3,0:T(2,128)(2,1)S(1)} %bitcast.11) | data formatting | bytes 2097152 | tf_op jit(solution)/shard_map/transpose | solution.py:523
  (4 shorter events, 0.0 us)
Async XLA Ops:
  4.1 1.9 %copy-start = (bf16[3,3,3,192,64]{3,4,2,1,0:T(8,128)(2,1)S(1)}, bf16[3,3,3,192,64]{3,4,2,1,0:T(8,128)(2,1)}, u32[]{:S(2)}) copy-start(bf16[3,3,3,192,64]{3,4,2,1,0:T(8,128)(2,1)} %param.20) | copy-start | bytes 1990660
  4.1 3.4 %copy-start.2 = (f32[64]{0:T(128)S(1)}, f32[64]{0:T(128)}, u32[]{:S(2)}) copy-start(f32[64]{0:T(128)} %param.13) | copy-start | bytes 772
  4.1 3.5 %copy-start.3 = (f32[64]{0:T(128)S(1)}, f32[64]{0:T(128)}, u32[]{:S(2)}) copy-start(f32[64]{0:T(128)} %param.21) | copy-start | bytes 772
  4.1 3.6 %copy-start.4 = (f32[128]{0:T(128)S(1)}, f32[128]{0:T(128)}, u32[]{:S(2)}) copy-start(f32[128]{0:T(128)} %param.15) | copy-start | bytes 1540
  4.1 3.6 %copy-start.5 = (f32[128]{0:T(128)S(1)}, f32[128]{0:T(128)}, u32[]{:S(2)}) copy-start(f32[128]{0:T(128)} %param.19) | copy-start | bytes 1540
  4.1 3.6 %copy-start.1 = (f32[256]{0:T(256)S(1)}, f32[256]{0:T(256)}, u32[]{:S(2)}) copy-start(f32[256]{0:T(256)} %param.17) | copy-start | bytes 3076
where the time goes:
time: 89.4 us; the launch traced here: 89.2 us
  Pallas kernels  73.8 us (83%)
  local copies, waits for them, and re-layouts  15.3 us (17%)
    pallas_call x1, Pallas kernels, on_device(): pl.pallas_call(functools.partial(kernel, sizes), out_shape=jax.ShapeDtype...  73.8 us
    reshape x2, local copies, waits for them, and re-layouts, on_device(): volume.reshape(NXF, ROWS, 2, 8, 2, 64).transpose(0, 3, 4, 1, 2, 5)  5.83 us
    reshape x1, local copies, waits for them, and re-layouts, on_device(): result.reshape(NXF, 8, ROWS, 2, 2, 64).transpose(0, 2, 4, 1, 3, 5)  3.99 us
    transpose x1, local copies, waits for them, and re-layouts, on_device(): result.reshape(NXF, 8, ROWS, 2, 2, 64).transpose(0, 2, 4, 1, 3, 5)  3.13 us

commit v1 on v0

v1 whole, which is shorter than its diff:
```python
import functools

import jax
import jax.numpy as jnp
from jax import lax
from jax.experimental import pallas as pl
from jax.experimental.pallas import tpu as pltpu
from jax.sharding import PartitionSpec as P

BF = jnp.bfloat16
F32 = jnp.float32
MESH = pl.DeviceIdType.MESH

NXF, NZF, ROWS = 16, 16, 16
NXM, NZM = 8, 8
TF, TM = 336, 112
LEVELS = 6
PEERS = [(x, 0, z) for x in (-1, 0, 1) for z in (-1, 0, 1) if x or z] + [(0, -1, 0), (0, 1, 0)]


def dot(a, b):
    return jnp.dot(a, b, preferred_element_type=F32)


def cells(ref, *index):
    value = ref[index]
    return value.reshape(-1, value.shape[-1])


def kernel(
    sizes,
    vol, wf_hbm, wm_hbm, wb_hbm, wrm_hbm, wrf_hbm, bf_ref, bm_ref, bb_ref, brm_ref, brf_ref,
    out_hbm,
    r_in, h_in, s_fine, y_in, yr_in,
    r_enc, h_enc, y_enc, yr_enc,
    r_pool, h_pool, s_pool, y_pool, yr_pool,
    r_mid, hu_mid, hd_mid, s_mid, y_mid, yr_mid,
    r_low, s_low, y_low, yr_low, pair_tmp,
    low_lanes, bottom_tmp, s_up, up_lanes,
    r_dec, hu_dec, hd_dec, s_dec, y_dec, yr_dec,
    wf_raw, wrf_raw, wrm_raw,
    w_fine, w_skip, w_mid, w_bottom, w_rm_skip, w_rm_up, w_rf_up,
    skip, vol_v, out_v, turn,
    send_sem, recv_sem, local_sem,
):
    spots = {axis: lax.axis_index(axis) for axis in ("gx", "gy", "gz")}

    def near(steps):
        return {
            axis: lax.rem(spots[axis] + (step + sizes[axis]), sizes[axis]) for axis, step in zip(sizes, steps) if step
        }

    def at_low(axis):
        return spots[axis] == 0

    def at_high(axis):
        return spots[axis] == sizes[axis] - 1

    def message(number, src, dst, *steps):
        return pltpu.make_async_remote_copy(
            src_ref=src, dst_ref=dst, send_sem=send_sem.at[number], recv_sem=recv_sem.at[number],
            device_id=near(steps), device_id_type=MESH,
        )

    sent = []

    def start(copies):
        for copy in copies:
            copy.start()
        sent.extend(copies)
        return copies

    def arrived(copies):
        for copy in copies:
            copy.wait_recv()

    loads = {}

    def load(name, src, dst):
        copy = pltpu.make_async_copy(src, dst, local_sem.at[len(loads)])
        copy.start()
        loads[name] = copy

    load("vol", vol, vol_v)
    load("wf", wf_hbm, wf_raw)
    load("wrf", wrf_hbm, wrf_raw)
    for dz in range(2):
        lanes = pl.ds(dz * 128, 128)
        for q, slot in ((1, 0), (2, 2), (0, 3)):
            load(("wm", dz, q), wm_hbm.at[:, q], w_mid.at[:, dz:dz + 3, slot, :, lanes])
    for q, slot in ((1, 0), (2, 1), (0, 2)):
        load(("wb", q), wb_hbm.at[:, q], w_bottom.at[:, :, slot])
    for dz in range(2):
        lanes = pl.ds(dz * 128, 128)
        for q, slot in ((1, 0), (2, 1), (0, 2)):
            load(("wrm", dz, q), wrm_hbm.at[:, q, :, 0:128, :], w_rm_skip.at[:, dz:dz + 3, slot, :, lanes])
    load("wrm_raw", wrm_hbm.at[:, :, :, 128:384, :], wrm_raw)

    barrier = pltpu.get_barrier_semaphore()
    for peer in PEERS:
        pl.semaphore_signal(barrier, inc=1, device_id=near(peer), device_id_type=MESH)
    pl.semaphore_wait(barrier, len(PEERS))

    def start_xz(base, ref, depth):
        depths = depth if isinstance(depth, tuple) else (depth, depth)
        nx, nz = ref.shape[0] - 2 * depths[0], ref.shape[1] - 2 * depths[1]

        def part(n, side, depth):
            own, rim = pl.ds(depth, n), pl.ds(depth, depth)
            if side == 0:
                return own, own
            if side < 0:
                return rim, pl.ds(n + depth, depth)
            return pl.ds(n, depth), pl.ds(0, depth)

        copies = []
        for number, (dx, dz) in enumerate(((-1, -1), (-1, 1), (1, -1), (1, 1), (-1, 0), (1, 0), (0, -1), (0, 1))):
            (src_x, dst_x), (src_z, dst_z) = part(nx, dx, depths[0]), part(nz, dz, depths[1])
            copies.append(message(base + number, ref.at[src_x, src_z], ref.at[dst_x, dst_z], dx, 0, dz))
        return start(copies)

    def clear_rim(ref, depth):
        dx, dz = depth if isinstance(depth, tuple) else (depth, depth)
        nx, nz = ref.shape[0], ref.shape[1]
        for edge, index in (
            (at_low("gx"), (pl.ds(0, dx),)), (at_high("gx"), (pl.ds(nx - dx, dx),)),
            (at_low("gz"), (pl.ds(0, nx), pl.ds(0, dz))), (at_high("gz"), (pl.ds(0, nx), pl.ds(nz - dz, dz))),
        ):
            @pl.when(edge)
            def _():
                ref[index] = jnp.zeros(ref.at[index].shape, BF)

    def wait_xz(copies, ref, s):
        arrived(copies)
        clear_rim(ref, 1)
        nx, nz = ref.shape[0], ref.shape[1]
        for plane in (0, nx - 1):
            s[plane, :, 8:24] = ref[plane].astype(F32)
        for plane in (0, nz - 1):
            s[1:nx - 1, plane, 8:24] = ref[1:nx - 1, plane].astype(F32)

    def start_y(base, s, ys, yr):
        count = ys.shape[1]
        rows = s.reshape(s.shape[0] * s.shape[1] * 32, 128)
        ys[0] = rows[pl.ds(8, count, stride=32), :].astype(BF)
        ys[1] = rows[pl.ds(23, count, stride=32), :].astype(BF)
        return start([
            message(base + 8, ys.at[0], yr.at[1], 0, -1, 0),
            message(base + 9, ys.at[1], yr.at[0], 0, 1, 0),
        ])

    def wait_y(copies, s, yr):
        arrived(copies)
        count = yr.shape[1]
        rows = s.reshape(s.shape[0] * s.shape[1] * 32, 128)
        low = jnp.where(at_low("gy"), 0.0, yr[0].astype(F32))
        high = jnp.where(at_high("gy"), 0.0, yr[1].astype(F32))
        rows[pl.ds(7, count, stride=32), :] = low
        rows[pl.ds(24, count, stride=32), :] = high

    def beside(s, dst, planes):
        lane = lax.broadcasted_iota(jnp.int32, dst.shape[1:], 2)

        def plane(x, carry):
            dst[x] = jnp.where(lane < 64, s[x, :, 9:25], s[x, :, 7:23]).astype(BF)
            return carry

        lax.fori_loop(0, planes, plane, 0)

    def beside_both(s, up, down, planes):
        def plane(x, carry):
            up[x] = s[x, :, 9:25].astype(BF)
            down[x] = s[x, :, 7:23].astype(BF)
            return carry

        lax.fori_loop(0, planes, plane, 0)

    def spread(raw, first, dst):
        dst[...] = jnp.zeros(dst.shape, BF)

        def one(p, carry):
            for r in range(3):
                taps = [raw[p, q, r, first:first + 64, :] for q in range(3)]
                none = jnp.zeros_like(taps[0])
                pairs = ((taps[1], taps[0]), (taps[2], taps[1]), (none, taps[2]), (taps[0], none))
                for slot, pair in enumerate(pairs):
                    block = jnp.concatenate(pair, axis=1)
                    for dz in range(2):
                        dst[p, r + dz, slot, :, dz * 128:(dz + 1) * 128] = block
            return carry

        lax.fori_loop(0, 3, one, 0)

    def fine_window(ref, side, x, count):
        ref, side = (value.reshape(NXF + 2, 9, 2, ROWS, 128) for value in (ref, side))
        parts = []
        for p in range(3):
            for zo in range(4):
                index = (pl.ds(x + p, count), pl.ds(zo // 2, 8), zo % 2)
                parts += [cells(ref, *index), cells(side, *index)]
        return jnp.concatenate(parts, axis=1)

    loads["vol"].wait()
    fine_rows = s_fine.reshape((NXF + 3) * (NZF + 2) * 32, 128)

    def turn_in(x, carry):
        for y in range(ROWS):
            pair = jnp.concatenate([vol_v[x, 2 * y], vol_v[x, 2 * y + 1]], axis=1)
            fine_rows[pl.ds(((x + 1) * (NZF + 2) + 1) * 32 + 8 + y, NZF, stride=32), :] = pair.astype(F32)
        r_in[x + 1, 1:NZF + 1] = s_fine[x + 1, 1:NZF + 1, 8:24].astype(BF)
        return carry

    lax.fori_loop(0, NXF, turn_in, 0)
    going = start_xz(0, r_in, 1)
    loads["wf"].wait()
    spread(wf_raw, 0, w_fine)
    w_mid[:, :, 1] = jnp.zeros((3, 4, 64, 256), BF)
    w_mid[:, 3, :, :, 0:128] = jnp.zeros((3, 4, 64, 128), BF)
    w_mid[:, 0, :, :, 128:256] = jnp.zeros((3, 4, 64, 128), BF)
    w_rm_skip[:, 3, :, :, 0:128] = jnp.zeros((3, 3, 128, 128), BF)
    w_rm_skip[:, 0, :, :, 128:256] = jnp.zeros((3, 3, 128, 128), BF)
    loads["wrf"].wait()
    spread(wrf_raw, 0, w_skip)
    wait_xz(going, r_in, s_fine)
    going = start_y(0, s_fine, y_in, yr_in)
    loads["wrm_raw"].wait()

    def sums(parts):
        return (parts[0], parts[1] + parts[2], parts[0] + parts[1], parts[2])

    def rise_mid(chunk, carry):
        rows = pl.ds(pl.multiple_of(chunk * 16, 16), 16)
        for q, slot in ((1, 0), (2, 1), (0, 2)):
            by_r = [sums([wrm_raw[p, q, r, rows, :].astype(F32) for p in range(3)]) for r in range(3)]
            for x_sum in range(4):
                z_sums = sums([by_r[r][x_sum] for r in range(3)])
                for z_sum, (zt, dz) in enumerate(((0, 0), (1, 0), (1, 1), (2, 1))):
                    w_rm_up[x_sum, zt, slot, rows, dz * 128:(dz + 1) * 128] = z_sums[z_sum].astype(BF)
        return carry

    w_rm_up[:, 0, :, :, 128:256] = jnp.zeros((4, 3, 256, 128), BF)
    w_rm_up[:, 2, :, :, 0:128] = jnp.zeros((4, 3, 256, 128), BF)
    lax.fori_loop(0, 16, rise_mid, 0)

    wait_y(going, s_fine, yr_in)
    beside(s_fine, h_in, NXF + 2)

    w_fine_all = w_fine.reshape(3072, 256)

    bias_fine = jnp.concatenate([bf_ref[...]] * 4, axis=1)
    bias_last = jnp.concatenate([brf_ref[...]] * 4, axis=1)
    r_enc_pairs = r_enc.reshape(NXF + 2, 9, 2, ROWS, 128)
    s_fine_pairs = s_fine.reshape(NXF + 3, 9, 2, 32, 128)
    r_pool_pairs = r_pool.reshape(NXM + 2, 5, 2, ROWS, 128)
    s_pool_pairs = s_pool.reshape(NXM + 4, 5, 2, 32, 128)

    def fine(pair, carry):
        x = 2 * pair
        result = dot(fine_window(r_in, h_in, x, 2), w_fine_all[...])
        result = jnp.maximum(result + bias_fine, 0.0).reshape(2, 8, ROWS, 256)
        for index, half in (((pl.ds(0, 8), 1), 0), ((pl.ds(1, 8), 0), 1)):
            value = result[..., half * 128:(half + 1) * 128]
            r_enc_pairs[(pl.ds(x + 1, 2),) + index] = value.astype(BF)
            s_fine_pairs[(pl.ds(x + 1, 2),) + index + (pl.ds(8, 16),)] = value
        most = jnp.max(result, axis=0)
        most = jnp.maximum(most[..., 0:128], most[..., 128:256]).reshape(128, 128)
        most = jnp.maximum(most, pltpu.roll(most, 64, 1)).reshape(4, 2, ROWS, 128)
        for index, half in (((pl.ds(0, 4), 1), 0), ((pl.ds(1, 4), 0), 1)):
            r_pool_pairs[(pair + 1,) + index] = most[:, half].astype(BF)
            s_pool_pairs[(pair + 1,) + index + (pl.ds(8, 16),)] = most[:, half]
        return carry

    lax.fori_loop(0, 8, fine, 0)

    going = start_xz(10, r_pool, 1)
    skipping = start_xz(20, r_enc, 1)

    def rise_fine(chunk, carry):
        src = pl.ds(pl.multiple_of(64 + chunk * 16, 16), 16)
        rows = pl.ds(pl.multiple_of(chunk * 16, 16), 16)
        by_q = []
        for q in range(3):
            by_r = [sums([wrf_raw[p, q, r, src, :].astype(F32) for p in range(3)]) for r in range(3)]
            by_q.append([sums([by_r[r][x_sum] for r in range(3)]) for x_sum in range(4)])
        none = jnp.zeros((16, 64), F32)
        for x_sum in range(4):
            for z_sum, (zt, dz) in enumerate(((0, 0), (1, 0), (1, 1), (2, 1))):
                taps = [by_q[q][x_sum][z_sum] for q in range(3)]
                pairs = ((taps[1] + taps[2], taps[0] + taps[1]), (none, taps[2]), (taps[0], none))
                for slot, pair in enumerate(pairs):
                    block = jnp.concatenate(pair, axis=1).astype(BF)
                    w_rf_up[x_sum, zt, slot, rows, dz * 128:(dz + 1) * 128] = block
        return carry

    w_rf_up[:, 0, :, :, 128:256] = jnp.zeros((4, 3, 128, 128), BF)
    w_rf_up[:, 2, :, :, 0:128] = jnp.zeros((4, 3, 128, 128), BF)
    lax.fori_loop(0, 8, rise_fine, 0)

    wait_xz(going, r_pool, s_pool)
    going = start_y(10, s_pool, y_pool, yr_pool)
    wait_xz(skipping, r_enc, s_fine)
    skipping = start_y(20, s_fine, y_enc, yr_enc)
    for dz in range(2):
        for q in range(3):
            loads[("wm", dz, q)].wait()
    wait_y(going, s_pool, yr_pool)
    beside(s_pool, h_pool, NXM + 2)

    parts = []
    for p in range(3):
        for zo in range(4):
            index = (pl.ds(p, 8), pl.ds(zo // 2, 4), zo % 2)
            parts += [cells(ref, *index) for ref in (r_pool_pairs, h_pool.reshape(NXM + 2, 5, 2, ROWS, 128))]
    result = dot(jnp.concatenate(parts, axis=1), w_mid.reshape(3072, 256)[...])
    r_mid_pairs, hu_mid_pairs, hd_mid_pairs, r_dec_pairs = (
        ref.reshape(5, 2, 5, 2, ROWS, 128) for ref in (r_mid, hu_mid, hd_mid, r_dec)
    )
    s_mid_pairs, s_dec_pairs = (ref.reshape(6, 2, 5, 2, 32, 128) for ref in (s_mid, s_dec))
    bias_mid = jnp.concatenate([bm_ref[...]] * 2, axis=1)
    bias_rise = jnp.concatenate([brm_ref[...]] * 2, axis=1)
    result = jnp.maximum(result + bias_mid, 0.0).reshape(4, 2, 4, ROWS, 256)
    for dz, index in enumerate(((pl.ds(0, 4), 1), (pl.ds(1, 4), 0))):
        value = result[..., dz * 128:(dz + 1) * 128]
        for dx in range(2):
            place = (pl.ds(0, 4), 1) if dx == 0 else (pl.ds(1, 4), 0)
            r_mid_pairs[place + index] = value[:, dx].astype(BF)
            s_mid_pairs[place + index + (pl.ds(8, 16),)] = value[:, dx]
    most = jnp.maximum(result[:, 0], result[:, 1])
    pair_tmp[...] = jnp.maximum(most[..., 0:128], most[..., 128:256]).reshape(256, 128)
    low = jnp.maximum(pair_tmp[pl.ds(0, 128, stride=2), :], pair_tmp[pl.ds(1, 128, stride=2), :])
    r_low[2:6, 1:3] = low.astype(BF).reshape(4, 2, ROWS, 128)

    going = start_xz(30, r_low, (2, 1))
    middle = start_xz(40, r_mid, 1)

    wait_y(skipping, s_fine, yr_enc)
    beside(s_fine, h_enc, NXF + 2)
    w_skip_all = w_skip.reshape(3072, 256)

    def skip_part(pair, carry):
        x = 2 * pair
        result = dot(fine_window(r_enc, h_enc, x, 2), w_skip_all[...]) + bias_last
        skip[pl.ds(x, 2)] = result.reshape(2, 128, 256)
        return carry

    lax.fori_loop(0, 3, skip_part, 0)
    arrived(going)
    clear_rim(r_low, (2, 1))
    low = r_low[...].astype(F32).reshape(8, 4, 2, 8, 128).reshape(8, 8, 8, 128)
    s_low[:, :, 8:16] = low
    s_low[:, :, 0:8] = jnp.zeros_like(low)
    s_low[:, :, 16:24] = jnp.zeros_like(low)
    rows = s_low.reshape(2048, 128)
    for number, row in enumerate((8, 9, 14, 15)):
        y_low[number // 2, pl.ds((number % 2) * 64, 64), :] = rows[pl.ds(row, 64, stride=32), :].astype(BF)
    going = start([
        message(38, y_low.at[0], yr_low.at[1], 0, -1, 0),
        message(39, y_low.at[1], yr_low.at[0], 0, 1, 0),
    ])
    wait_xz(middle, r_mid, s_mid)
    middle = start_y(40, s_mid, y_mid, yr_mid)
    for q in range(3):
        loads[("wb", q)].wait()
    lax.fori_loop(3, 5, skip_part, 0)
    arrived(going)
    for number, row in enumerate((6, 7, 16, 17)):
        edge = at_low("gy") if number < 2 else at_high("gy")
        value = yr_low[number // 2, pl.ds((number % 2) * 64, 64), :].astype(F32)
        rows[pl.ds(row, 64, stride=32), :] = jnp.where(edge, 0.0, value)

    def low_plane(x, carry):
        for slot, first in enumerate((4, 5, 3)):
            low_lanes[x, :, :, slot * 128:(slot + 1) * 128] = s_low[x, :, first:first + 16].astype(BF)
        return carry

    lax.fori_loop(0, 8, low_plane, 0)
    parts = [cells(low_lanes, pl.ds(p, 6), pl.ds(r, 6)) for p in range(3) for r in range(3)]
    result = dot(jnp.concatenate(parts, axis=1), w_bottom.reshape(3456, 256)[...])
    result = jnp.maximum(result + bb_ref[...], 0.0).reshape(6, 6, ROWS, 256)
    index = lax.broadcasted_iota(jnp.int32, (6, 6, ROWS, 256), 0)
    zindex = lax.broadcasted_iota(jnp.int32, (6, 6, ROWS, 256), 1)
    yindex = lax.broadcasted_iota(jnp.int32, (6, 6, ROWS, 256), 2)
    outside = False
    for where, first, last, axis in ((index, 0, 5, "gx"), (zindex, 0, 5, "gz"), (yindex, 3, 12, "gy")):
        outside = outside | ((where == first) & at_low(axis)) | ((where == last) & at_high(axis))
    result = jnp.where(outside, 0.0, result).reshape(576, 256)
    for half in range(2):
        bottom_tmp[half] = result[:, half * 128:(half + 1) * 128]

    for half in range(2):
        doubled = s_up.at[half].reshape(36 * 32, 128)
        for step in range(10):
            value = bottom_tmp.at[half][pl.ds(3 + step, 36, stride=16), :]
            doubled[pl.ds(6 + 2 * step, 36, stride=32), :] = value
            doubled[pl.ds(7 + 2 * step, 36, stride=32), :] = value
    for slot, first in enumerate((8, 9, 7)):
        for half in range(2):
            lanes = slice(slot * 256 + half * 128, slot * 256 + half * 128 + 128)
            up_lanes[:, :, :, lanes] = s_up[half, :, first:first + 16].astype(BF).reshape(6, 6, ROWS, 128)

    wait_y(middle, s_mid, yr_mid)
    beside_both(s_mid, hu_mid, hd_mid, NXM + 2)
    for dz in range(2):
        for q in range(3):
            loads[("wrm", dz, q)].wait()

    for dx in range(2):
        parts = []
        for p in range(3):
            for zo in range(4):
                index = (pl.ds((dx + p) // 2, 4), (dx + p) % 2, pl.ds(zo // 2, 4), zo % 2)
                parts += [cells(ref, *index) for ref in (r_mid_pairs, hu_mid_pairs, hd_mid_pairs)]
        result = dot(jnp.concatenate(parts, axis=1), w_rm_skip.reshape(4608, 256)[...])
        parts = []
        for xt in range(2):
            for zt in range(3):
                parts.append(cells(up_lanes, pl.ds(xt + dx, 4), pl.ds(zt, 4)))
        weight = w_rm_up.reshape(2, 4608, 256)[dx]
        result = result + dot(jnp.concatenate(parts, axis=1), weight)
        result = jnp.maximum(result + bias_rise, 0.0).reshape(4, 4, ROWS, 256)
        for dz, index in enumerate(((pl.ds(0, 4), 1), (pl.ds(1, 4), 0))):
            place = (pl.ds(0, 4), 1) if dx == 0 else (pl.ds(1, 4), 0)
            value = result[..., dz * 128:(dz + 1) * 128]
            r_dec_pairs[place + index] = value.astype(BF)
            s_dec_pairs[place + index + (pl.ds(8, 16),)] = value

    going = start_xz(50, r_dec, 1)
    lax.fori_loop(5, 7, skip_part, 0)
    wait_xz(going, r_dec, s_dec)
    going = start_y(50, s_dec, y_dec, yr_dec)
    lax.fori_loop(7, 8, skip_part, 0)
    wait_y(going, s_dec, yr_dec)
    beside_both(s_dec, hu_dec, hd_dec, NXM + 2)

    weight = w_rf_up.reshape(2, 2304, 256)
    turn_rows = turn.reshape(4 * NZF * ROWS, 128)

    def leave(step):
        planes = pl.ds(4 * step, 4)
        return pltpu.make_async_copy(out_v.at[planes], out_hbm.at[planes], local_sem.at[len(loads) + step])

    def last(step, carry):
        x = 2 * step
        for dx in range(2):
            parts = []
            for xt in range(2):
                for zt in range(3):
                    parts += [cells(ref, pl.ds(x + xt + dx, 2), pl.ds(zt, 8)) for ref in (r_dec, hu_dec, hd_dec)]
            result = dot(jnp.concatenate(parts, axis=1), weight[dx]).reshape(2, 128, 256)
            for i in range(2):
                value = (result[i] + skip[4 * step + 2 * i + dx]).reshape(8, ROWS, 256)
                for dz in range(2):
                    turn[2 * i + dx, :, dz] = value[..., dz * 128:(dz + 1) * 128]
        for i in range(4):
            for y in range(ROWS):
                value = turn_rows[pl.ds(i * NZF * ROWS + y, NZF, stride=ROWS), :].astype(BF)
                out_v[4 * step + i, 2 * y] = value[:, 0:64]
                out_v[4 * step + i, 2 * y + 1] = value[:, 64:128]
        leave(step).start()
        return carry

    lax.fori_loop(0, 4, last, 0)
    for message_sent in sent:
        message_sent.wait_send()
    for step in range(4):
        leave(step).wait()


def scratch():
    vmem = pltpu.VMEM
    fine = (NXF + 2, NZF + 2, ROWS, 128)
    mid = pool = (NXM + 2, NZM + 2, ROWS, 128)
    mid_s = (NXM + 4, NZM + 2, 32, 128)
    return [
        vmem(fine, BF), vmem(fine, BF), vmem((NXF + 3, NZF + 2, 32, 128), F32), vmem((2, TF, 128), BF), vmem((2, TF, 128), BF),
        vmem(fine, BF), vmem(fine, BF), vmem((2, TF, 128), BF), vmem((2, TF, 128), BF),
        vmem(pool, BF), vmem(pool, BF), vmem(mid_s, F32), vmem((2, TM, 128), BF), vmem((2, TM, 128), BF),
        vmem(mid, BF), vmem(mid, BF), vmem(mid, BF), vmem(mid_s, F32), vmem((2, TM, 128), BF), vmem((2, TM, 128), BF),
        vmem((8, 4, ROWS, 128), BF), vmem((8, 8, 32, 128), F32), vmem((2, 128, 128), BF), vmem((2, 128, 128), BF),
        vmem((256, 128), F32),
        vmem((8, 8, ROWS, 384), BF), vmem((2, 576, 128), F32), vmem((2, 36, 32, 128), F32), vmem((6, 6, ROWS, 768), BF),
        vmem(mid, BF), vmem(mid, BF), vmem(mid, BF), vmem(mid_s, F32), vmem((2, TM, 128), BF), vmem((2, TM, 128), BF),
        vmem((3, 3, 3, 64, 64), BF), vmem((3, 3, 3, 192, 64), BF), vmem((3, 3, 3, 256, 128), BF),
        vmem((3, 4, 4, 64, 256), BF), vmem((3, 4, 4, 64, 256), BF), vmem((3, 4, 4, 64, 256), BF),
        vmem((3, 3, 3, 128, 256), BF), vmem((3, 4, 3, 128, 256), BF), vmem((4, 3, 3, 256, 256), BF),
        vmem((4, 3, 3, 128, 256), BF),
        vmem((NXF, 128, 256), F32), vmem((NXF, 32, NZF, 64), BF), vmem((NXF, 32, NZF, 64), BF),
        vmem((4, 8, 2, ROWS, 128), F32),
        pltpu.SemaphoreType.DMA((10 * LEVELS,)), pltpu.SemaphoreType.DMA((10 * LEVELS,)), pltpu.SemaphoreType.DMA((32,)),
    ]


def on_device(sizes, volume, wf, bf, wm, bm, wb, bb, wrm, brm, wrf, brf):
    hbm = pl.BlockSpec(memory_space=pl.ANY)
    return pl.pallas_call(
        functools.partial(kernel, sizes),
        out_shape=jax.ShapeDtypeStruct((NXF, 32, NZF, 64), BF),
        in_specs=[hbm] * 6 + [pl.BlockSpec(memory_space=pltpu.VMEM)] * 5,
        out_specs=hbm,
        scratch_shapes=scratch(),
        compiler_params=pltpu.CompilerParams(
            collective_id=0, has_side_effects=True, vmem_limit_bytes=62 * 2**20
        ),
    )(volume, wf, wm, wb, wrm, wrf, *(bias.reshape(1, -1) for bias in (bf, bm, bb, brm, brf)))


def solution(mesh):
    return jax.shard_map(
        functools.partial(on_device, dict(mesh.shape)),
        mesh=mesh,
        in_specs=(P("gx", "gy", "gz", None),) + (P(),) * 10,
        out_specs=P("gx", "gy", "gz", None),
        check_vma=False,
    )
```

time: 89.4 us -> 72.7 us (0.81)
  local copies, waits for them, and re-layouts: 15.3 us -> 5.78 us
  Pallas kernels: 73.8 us -> 66.8 us
    reshape x3 -> x0, local copies, waits for them, and re-layouts: 9.82 us -> none  [the longest x2 5.83 us: on_device(): volume.reshape(NXF, ROWS, 2, 8, 2, 64).transpose(0, 3, 4, 1, 2, 5)]
    pallas_call x1, Pallas kernels: 73.8 us -> 66.8 us  [on_device(): pl.pallas_call(functools.partial(kernel, sizes), out_shape=jax.ShapeDtype...]
    unnamed x13 -> x2, local copies, waits for them, and re-layouts: 1.61 us -> 5.78 us
    transpose x1 -> x0, local copies, waits for them, and re-layouts: 3.13 us -> none  [on_device(): result.reshape(NXF, 8, ROWS, 2, 2, 64).transpose(0, 2, 4, 1, 3, 5)]
where the time goes in v1:
time: 72.7 us; the launch traced here: 72.6 us
  Pallas kernels  66.8 us (92%)
  local copies, waits for them, and re-layouts  5.78 us (8%)
    pallas_call x1, Pallas kernels, on_device(): pl.pallas_call(functools.partial(kernel, sizes), out_shape=jax.ShapeDtype...  66.8 us
    unnamed x2, local copies, waits for them, and re-layouts  5.78 us

profile of v1, /device:TPU:2, one launch (start us, length us, event | category | flops | bytes accessed | tf_op | source)
XLA Modules:
  0.0 72.6 jit_solution(3109021233399189373)
XLA Ops:
  0.0 2.4 %copy.12.wrf_hbm = bf16[3,3,3,192,64]{4,3,2,1,0:T(8,128)(2,1)} copy(bf16[3,3,3,192,64]{3,4,2,1,0:T(8,128)(2,1)} %param.20) | data formatting | bytes 1327104 | tf_op args[9]
  2.4 66.8 %shard_map.109 = bf16[16,32,16,64]{3,2,1,0:T(8,128)(2,1)} custom-call(bf16[16,32,16,64]{3,2,1,0:T(8,128)(2,1)} %vol.1, bf16[3,3,3,64,64]{4,3,2,1,0:T(8,128)(2,1)} %wf_hbm.1, bf16[3,3,3,64,128]{4,3,2,1,0:T(8,128)(2,1)} %wm_hbm.1, bf16[3,3,3,128,256]{4,3,2,1,0:T(8,128)(2,1)} %wb_hbm.1, bf16[3,3,3,384,128]{4,3,2,1,0:T(8,128)(2,1)} %wrm_hbm.1, ...), custom_call_target="tpu_custom_call" | custom-call | tf_op jit(solution)/shard_map/pallas_call | solution.py:495
  69.2 3.4 %copy.14 = bf16[16,32,16,64]{3,2,1,0:T(8,128)(2,1)} copy(bf16[16,32,16,64]{3,2,1,0:T(8,128)(2,1)} %shard_map.109) | data formatting | bytes 2097152

commit v2 on v1

--- a/solution.py
+++ b/solution.py
@@ -13,7 +13,7 @@
 
 NXF, NZF, ROWS = 16, 16, 16
 NXM, NZM = 8, 8
-TF, TM = 336, 112
+TF, TM = 352, 112
 LEVELS = 6
 PEERS = [(x, 0, z) for x in (-1, 0, 1) for z in (-1, 0, 1) if x or z] + [(0, -1, 0), (0, 1, 0)]
 
@@ -30,17 +30,18 @@
 def kernel(
     sizes,
     vol, wf_hbm, wm_hbm, wb_hbm, wrm_hbm, wrf_hbm, bf_ref, bm_ref, bb_ref, brm_ref, brf_ref,
-    out_hbm,
-    r_in, h_in, s_fine, y_in, yr_in,
-    r_enc, h_enc, y_enc, yr_enc,
+    out_v,
+    r_in, h_in, rim_in, side_in, y_in, yr_in,
+    r_enc, h_enc, rim_enc, side_enc, y_enc, yr_enc,
+    s_fine, s_rim, y_wide, y_grid, y_window,
     r_pool, h_pool, s_pool, y_pool, yr_pool,
     r_mid, hu_mid, hd_mid, s_mid, y_mid, yr_mid,
     r_low, s_low, y_low, yr_low, pair_tmp,
     low_lanes, bottom_tmp, s_up, up_lanes,
-    r_dec, hu_dec, hd_dec, s_dec, y_dec, yr_dec,
+    r_dec, hu_dec, hd_dec, rim_dec, up_dec, down_dec, y_dec, yr_dec, s_dec, s_dec_rim, y_dec_wide, y_dec_grid, y_dec_window,
     wf_raw, wrf_raw, wrm_raw,
     w_fine, w_skip, w_mid, w_bottom, w_rm_skip, w_rm_up, w_rf_up,
-    skip, vol_v, out_v, turn,
+    acc, vol_v,
     send_sem, recv_sem, local_sem,
 ):
     spots = {axis: lax.axis_index(axis) for axis in ("gx", "gy", "gz")}
@@ -96,6 +97,20 @@
             load(("wrm", dz, q), wrm_hbm.at[:, q, :, 0:128, :], w_rm_skip.at[:, dz:dz + 3, slot, :, lanes])
     load("wrm_raw", wrm_hbm.at[:, :, :, 128:384, :], wrm_raw)
 
+    for ref in (r_in, h_in, r_enc, h_enc, r_dec, hu_dec, hd_dec):
+        nx, nz = ref.shape[0], ref.shape[1]
+        for plane in (0, nx - 1):
+            ref[plane] = jnp.zeros(ref.shape[1:], BF)
+        for plane in (0, nz - 1):
+            ref[:, plane] = jnp.zeros((nx, ROWS, 128), BF)
+    for ref in (rim_in, rim_enc, rim_dec, side_in, side_enc, up_dec, down_dec):
+        for end in (0, ref.shape[1] - 1):
+            ref[0:2, end] = jnp.zeros((2, ROWS, 128), BF)
+    for ref, count in ((s_fine, 256), (s_dec, 64), (s_rim, 96), (s_dec_rim, 48)):
+        rows = ref.reshape(count * 32, 128)
+        for row in (7, 24):
+            rows[pl.ds(row, count, stride=32), :] = jnp.zeros((count, 128), F32)
+
     barrier = pltpu.get_barrier_semaphore()
     for peer in PEERS:
         pl.semaphore_signal(barrier, inc=1, device_id=near(peer), device_id_type=MESH)
@@ -158,6 +173,75 @@
         rows[pl.ds(7, count, stride=32), :] = low
         rows[pl.ds(24, count, stride=32), :] = high
 
+    def start_rims(base, ref, rim):
+        nx, nz = ref.shape[0] - 2, ref.shape[1] - 2
+        own_x, own_z = pl.ds(1, nx), pl.ds(1, nz)
+        return start([
+            message(base, ref.at[1, 1], rim.at[3, nx + 1], -1, 0, -1),
+            message(base + 1, ref.at[1, nz], rim.at[2, nx + 1], -1, 0, 1),
+            message(base + 2, ref.at[nx, 1], rim.at[3, 0], 1, 0, -1),
+            message(base + 3, ref.at[nx, nz], rim.at[2, 0], 1, 0, 1),
+            message(base + 4, ref.at[1, own_z], rim.at[1, own_z], -1, 0, 0),
+            message(base + 5, ref.at[nx, own_z], rim.at[0, own_z], 1, 0, 0),
+            message(base + 6, ref.at[own_x, 1], rim.at[3, own_x], 0, 0, -1),
+            message(base + 7, ref.at[own_x, nz], rim.at[2, own_x], 0, 0, 1),
+        ])
+
+    def wait_rims(copies, rim, s):
+        arrived(copies)
+        n = rim.shape[1] - 2
+        empty = jnp.zeros((n + 2, ROWS, 128), BF)
+        for edge, side, end in (
+            (at_low("gx"), 0, 0), (at_high("gx"), 1, n + 1), (at_low("gz"), 2, None), (at_high("gz"), 3, None),
+        ):
+            @pl.when(edge)
+            def _():
+                rim[side] = empty
+                if end is not None:
+                    rim[2:4, end] = empty[0:2]
+
+        s[0:n, 8:24] = rim[0, 1:n + 1].astype(F32)
+        s[n:2 * n, 8:24] = rim[1, 1:n + 1].astype(F32)
+        s[2 * n:3 * n + 2, 8:24] = rim[2].astype(F32)
+        s[4 * n:5 * n + 2, 8:24] = rim[3].astype(F32)
+
+    def start_rows(base, s, s_side, ys, yr):
+        count, more = s.shape[0] * s.shape[1], s_side.shape[0]
+        rows, side_rows = s.reshape(count * 32, 128), s_side.reshape(more * 32, 128)
+        for number, row in enumerate((8, 23)):
+            ys[number, 0:count] = rows[pl.ds(row, count, stride=32), :].astype(BF)
+            ys[number, count:count + more] = side_rows[pl.ds(row, more, stride=32), :].astype(BF)
+        return start([
+            message(base + 8, ys.at[0], yr.at[1], 0, -1, 0),
+            message(base + 9, ys.at[1], yr.at[0], 0, 1, 0),
+        ])
+
+    def wait_rows(copies, s_side, yr, wide, grid, window, step):
+        arrived(copies)
+        more = s_side.shape[0]
+        count = yr.shape[1] - more
+        n = grid.shape[1] - 2
+        for number, edge in enumerate((at_low("gy"), at_high("gy"))):
+            value = jnp.where(edge, 0.0, yr[number].astype(F32))
+            wide[number] = value
+            grid[number, 1:n + 1, 8:8 + n] = value[0:count].reshape(n, n, 128)
+            grid[number, 0, 8:8 + n] = value[count:count + n]
+            grid[number, n + 1, 8:8 + n] = value[count + n:count + 2 * n]
+            flat = grid.at[number].reshape((n + 2) * 32, 128)
+            flat[pl.ds(7, n + 2, stride=32), :] = wide[number, count + 2 * n:count + 3 * n + 2]
+            flat[pl.ds(8 + n, n + 2, stride=32), :] = wide[number, count + 4 * n:count + 5 * n + 2]
+
+            def gather(x, carry):
+                for tap in range(window.shape[1]):
+                    window[number, tap, x] = flat[pl.ds(x * 32 + 7 + tap, 8, stride=step), :]
+                return carry
+
+            lax.fori_loop(0, n + 2, gather, 0)
+
+    def select_rows(s, index):
+        lane = lax.broadcasted_iota(jnp.int32, (ROWS, 128), 1)
+        return jnp.where(lane < 64, s[index + (slice(9, 25),)], s[index + (slice(7, 23),)]).astype(BF)
+
     def beside(s, dst, planes):
         lane = lax.broadcasted_iota(jnp.int32, dst.shape[1:], 2)
 
@@ -200,20 +284,82 @@
                 parts += [cells(ref, *index), cells(side, *index)]
         return jnp.concatenate(parts, axis=1)
 
+    acc_rows = acc.reshape(NXF * 8 * 2 * ROWS, 128)
+    halves = ((0, slice(0, 128)), (1, slice(128, 256)))
+
+    def fine_own(ref, side, weight, first, last):
+        def step(pair, carry):
+            x = 2 * pair
+            result = dot(fine_window(ref, side, x, 2), weight.reshape(3072, 256)[...])
+            for dz, lanes in halves:
+                acc[pl.ds(x, 2), :, dz] = result[:, lanes].reshape(2, 8, ROWS, 128)
+            return carry
+
+        lax.fori_loop(first, last, step, 0)
+
+    def fine_sides(ref, side):
+        def plane(x, carry):
+            side[x + 1, 1:NZF + 1] = select_rows(ref, (x, slice(None)))
+            return carry
+
+        lax.fori_loop(0, NXF, plane, 0)
+
+    def fine_rims(rim, side, weight):
+        n = NXF
+        side[0, 1:n + 1] = select_rows(s_rim, (slice(0, n),))
+        side[1, 1:n + 1] = select_rows(s_rim, (slice(n, 2 * n),))
+        side[2] = select_rows(s_rim, (slice(2 * n, 3 * n + 2),))
+        side[3] = select_rows(s_rim, (slice(4 * n, 5 * n + 2),))
+        rim_pairs, side_pairs = (value.reshape(4, 9, 2, ROWS, 128) for value in (rim, side))
+        for low_high, x, p in ((0, 0, 0), (1, NXF - 1, 2)):
+            parts = []
+            for zo in range(4):
+                index = (low_high, pl.ds(zo // 2, 8), zo % 2)
+                parts += [cells(rim_pairs, *index), cells(side_pairs, *index)]
+            result = dot(jnp.concatenate(parts, axis=1), weight[p].reshape(1024, 256))
+            for dz, lanes in halves:
+                acc[x, :, dz] += result[:, lanes].reshape(8, ROWS, 128)
+        for low_high, z, zo in ((2, 0, 0), (3, 7, 3)):
+            parts = []
+            for p in range(3):
+                parts += [cells(rim, low_high, pl.ds(p, NXF)), cells(side, low_high, pl.ds(p, NXF))]
+            result = dot(jnp.concatenate(parts, axis=1), weight[:, zo].reshape(768, 256))
+            for dz, lanes in halves:
+                acc[:, z, dz] += result[:, lanes].reshape(NXF, ROWS, 128)
+
+    def fine_ends(weight):
+        lane = lax.broadcasted_iota(jnp.int32, (128, 128), 1)
+        for number, row in ((0, 0), (1, ROWS - 1)):
+            used = (lane >= 64) if number == 0 else (lane < 64)
+            parts = []
+            for p in range(3):
+                for zo in range(4):
+                    value = y_window[number, zo, p:p + NXF].reshape(128, 128)
+                    parts.append(jnp.where(used, value, 0.0).astype(BF))
+            result = dot(jnp.concatenate(parts, axis=1), weight[:, :, 2:4].reshape(1536, 256))
+            for dz, lanes in halves:
+                acc_rows[pl.ds(dz * ROWS + row, 128, stride=32), :] += result[:, lanes]
+
     loads["vol"].wait()
-    fine_rows = s_fine.reshape((NXF + 3) * (NZF + 2) * 32, 128)
+    fine_rows = s_fine.reshape(NXF * NZF * 32, 128)
 
     def turn_in(x, carry):
         for y in range(ROWS):
             pair = jnp.concatenate([vol_v[x, 2 * y], vol_v[x, 2 * y + 1]], axis=1)
-            fine_rows[pl.ds(((x + 1) * (NZF + 2) + 1) * 32 + 8 + y, NZF, stride=32), :] = pair.astype(F32)
-        r_in[x + 1, 1:NZF + 1] = s_fine[x + 1, 1:NZF + 1, 8:24].astype(BF)
+            fine_rows[pl.ds(x * NZF * 32 + 8 + y, NZF, stride=32), :] = pair.astype(F32)
+        r_in[x + 1, 1:NZF + 1] = s_fine[x, :, 8:24].astype(BF)
         return carry
 
     lax.fori_loop(0, NXF, turn_in, 0)
-    going = start_xz(0, r_in, 1)
+    going = start_rims(0, r_in, rim_in)
+    fine_sides(s_fine, h_in)
     loads["wf"].wait()
     spread(wf_raw, 0, w_fine)
+    fine_own(r_in, h_in, w_fine, 0, 6)
+    wait_rims(going, rim_in, s_rim)
+    going = start_rows(0, s_fine, s_rim, y_in, yr_in)
+    fine_own(r_in, h_in, w_fine, 6, 8)
+    fine_rims(rim_in, side_in, w_fine)
     w_mid[:, :, 1] = jnp.zeros((3, 4, 64, 256), BF)
     w_mid[:, 3, :, :, 0:128] = jnp.zeros((3, 4, 64, 128), BF)
     w_mid[:, 0, :, :, 128:256] = jnp.zeros((3, 4, 64, 128), BF)
@@ -221,8 +367,6 @@
     w_rm_skip[:, 0, :, :, 128:256] = jnp.zeros((3, 3, 128, 128), BF)
     loads["wrf"].wait()
     spread(wrf_raw, 0, w_skip)
-    wait_xz(going, r_in, s_fine)
-    going = start_y(0, s_fine, y_in, yr_in)
     loads["wrm_raw"].wait()
 
     def sums(parts):
@@ -242,28 +386,25 @@
     w_rm_up[:, 2, :, :, 0:128] = jnp.zeros((4, 3, 256, 128), BF)
     lax.fori_loop(0, 16, rise_mid, 0)
 
-    wait_y(going, s_fine, yr_in)
-    beside(s_fine, h_in, NXF + 2)
-
-    w_fine_all = w_fine.reshape(3072, 256)
-
-    bias_fine = jnp.concatenate([bf_ref[...]] * 4, axis=1)
-    bias_last = jnp.concatenate([brf_ref[...]] * 4, axis=1)
+    wait_rows(going, s_rim, yr_in, y_wide, y_grid, y_window, 2)
+    fine_ends(w_fine)
+
+    bias_fine = jnp.concatenate([bf_ref[...]] * 2, axis=1)
+    bias_last = jnp.concatenate([brf_ref[...]] * 2, axis=1)
     r_enc_pairs = r_enc.reshape(NXF + 2, 9, 2, ROWS, 128)
-    s_fine_pairs = s_fine.reshape(NXF + 3, 9, 2, 32, 128)
+    s_fine_pairs = s_fine.reshape(NXF, 8, 2, 32, 128)
     r_pool_pairs = r_pool.reshape(NXM + 2, 5, 2, ROWS, 128)
     s_pool_pairs = s_pool.reshape(NXM + 4, 5, 2, 32, 128)
 
     def fine(pair, carry):
         x = 2 * pair
-        result = dot(fine_window(r_in, h_in, x, 2), w_fine_all[...])
-        result = jnp.maximum(result + bias_fine, 0.0).reshape(2, 8, ROWS, 256)
-        for index, half in (((pl.ds(0, 8), 1), 0), ((pl.ds(1, 8), 0), 1)):
-            value = result[..., half * 128:(half + 1) * 128]
+        values = []
+        for dz, index in enumerate(((pl.ds(0, 8), 1), (pl.ds(1, 8), 0))):
+            value = jnp.maximum(acc[pl.ds(x, 2), :, dz] + bias_fine, 0.0)
             r_enc_pairs[(pl.ds(x + 1, 2),) + index] = value.astype(BF)
-            s_fine_pairs[(pl.ds(x + 1, 2),) + index + (pl.ds(8, 16),)] = value
-        most = jnp.max(result, axis=0)
-        most = jnp.maximum(most[..., 0:128], most[..., 128:256]).reshape(128, 128)
+            s_fine_pairs[pl.ds(x, 2), :, dz, 8:24] = value
+            values.append(value)
+        most = jnp.maximum(jnp.max(values[0], axis=0), jnp.max(values[1], axis=0)).reshape(128, 128)
         most = jnp.maximum(most, pltpu.roll(most, 64, 1)).reshape(4, 2, ROWS, 128)
         for index, half in (((pl.ds(0, 4), 1), 0), ((pl.ds(1, 4), 0), 1)):
             r_pool_pairs[(pair + 1,) + index] = most[:, half].astype(BF)
@@ -273,7 +414,9 @@
     lax.fori_loop(0, 8, fine, 0)
 
     going = start_xz(10, r_pool, 1)
-    skipping = start_xz(20, r_enc, 1)
+    skipping = start_rims(20, r_enc, rim_enc)
+    fine_sides(s_fine, h_enc)
+    fine_own(r_enc, h_enc, w_skip, 0, 4)
 
     def rise_fine(chunk, carry):
         src = pl.ds(pl.multiple_of(64 + chunk * 16, 16), 16)
@@ -298,8 +441,9 @@
 
     wait_xz(going, r_pool, s_pool)
     going = start_y(10, s_pool, y_pool, yr_pool)
-    wait_xz(skipping, r_enc, s_fine)
-    skipping = start_y(20, s_fine, y_enc, yr_enc)
+    wait_rims(skipping, rim_enc, s_rim)
+    skipping = start_rows(20, s_fine, s_rim, y_enc, yr_enc)
+    fine_own(r_enc, h_enc, w_skip, 4, 5)
     for dz in range(2):
         for q in range(3):
             loads[("wm", dz, q)].wait()
@@ -315,7 +459,8 @@
     r_mid_pairs, hu_mid_pairs, hd_mid_pairs, r_dec_pairs = (
         ref.reshape(5, 2, 5, 2, ROWS, 128) for ref in (r_mid, hu_mid, hd_mid, r_dec)
     )
-    s_mid_pairs, s_dec_pairs = (ref.reshape(6, 2, 5, 2, 32, 128) for ref in (s_mid, s_dec))
+    s_mid_pairs = s_mid.reshape(6, 2, 5, 2, 32, 128)
+    s_dec_pairs = s_dec.reshape(4, 2, 4, 2, 32, 128)
     bias_mid = jnp.concatenate([bm_ref[...]] * 2, axis=1)
     bias_rise = jnp.concatenate([brm_ref[...]] * 2, axis=1)
     result = jnp.maximum(result + bias_mid, 0.0).reshape(4, 2, 4, ROWS, 256)
@@ -333,17 +478,8 @@
     going = start_xz(30, r_low, (2, 1))
     middle = start_xz(40, r_mid, 1)
 
-    wait_y(skipping, s_fine, yr_enc)
-    beside(s_fine, h_enc, NXF + 2)
-    w_skip_all = w_skip.reshape(3072, 256)
-
-    def skip_part(pair, carry):
-        x = 2 * pair
-        result = dot(fine_window(r_enc, h_enc, x, 2), w_skip_all[...]) + bias_last
-        skip[pl.ds(x, 2)] = result.reshape(2, 128, 256)
-        return carry
-
-    lax.fori_loop(0, 3, skip_part, 0)
+    fine_own(r_enc, h_enc, w_skip, 5, 8)
+    fine_rims(rim_enc, side_enc, w_skip)
     arrived(going)
     clear_rim(r_low, (2, 1))
     low = r_low[...].astype(F32).reshape(8, 4, 2, 8, 128).reshape(8, 8, 8, 128)
@@ -361,7 +497,8 @@
     middle = start_y(40, s_mid, y_mid, yr_mid)
     for q in range(3):
         loads[("wb", q)].wait()
-    lax.fori_loop(3, 5, skip_part, 0)
+    wait_rows(skipping, s_rim, yr_enc, y_wide, y_grid, y_window, 2)
+    fine_ends(w_skip)
     arrived(going)
     for number, row in enumerate((6, 7, 16, 17)):
         edge = at_low("gy") if number < 2 else at_high("gy")
@@ -422,70 +559,107 @@
             place = (pl.ds(0, 4), 1) if dx == 0 else (pl.ds(1, 4), 0)
             value = result[..., dz * 128:(dz + 1) * 128]
             r_dec_pairs[place + index] = value.astype(BF)
-            s_dec_pairs[place + index + (pl.ds(8, 16),)] = value
-
-    going = start_xz(50, r_dec, 1)
-    lax.fori_loop(5, 7, skip_part, 0)
-    wait_xz(going, r_dec, s_dec)
-    going = start_y(50, s_dec, y_dec, yr_dec)
-    lax.fori_loop(7, 8, skip_part, 0)
-    wait_y(going, s_dec, yr_dec)
-    beside_both(s_dec, hu_dec, hd_dec, NXM + 2)
+            s_dec_pairs[:, dx, :, dz, 8:24] = value
+
+    going = start_rims(50, r_dec, rim_dec)
+
+    def dec_sides(x, carry):
+        hu_dec[x + 1, 1:NZM + 1] = s_dec[x, :, 9:25].astype(BF)
+        hd_dec[x + 1, 1:NZM + 1] = s_dec[x, :, 7:23].astype(BF)
+        return carry
+
+    lax.fori_loop(0, NXM, dec_sides, 0)
 
     weight = w_rf_up.reshape(2, 2304, 256)
-    turn_rows = turn.reshape(4 * NZF * ROWS, 128)
-
-    def leave(step):
-        planes = pl.ds(4 * step, 4)
-        return pltpu.make_async_copy(out_v.at[planes], out_hbm.at[planes], local_sem.at[len(loads) + step])
-
-    def last(step, carry):
+
+    def up_own(step, carry):
         x = 2 * step
         for dx in range(2):
             parts = []
             for xt in range(2):
                 for zt in range(3):
                     parts += [cells(ref, pl.ds(x + xt + dx, 2), pl.ds(zt, 8)) for ref in (r_dec, hu_dec, hd_dec)]
-            result = dot(jnp.concatenate(parts, axis=1), weight[dx]).reshape(2, 128, 256)
+            result = dot(jnp.concatenate(parts, axis=1), weight[dx])
             for i in range(2):
-                value = (result[i] + skip[4 * step + 2 * i + dx]).reshape(8, ROWS, 256)
-                for dz in range(2):
-                    turn[2 * i + dx, :, dz] = value[..., dz * 128:(dz + 1) * 128]
-        for i in range(4):
-            for y in range(ROWS):
-                value = turn_rows[pl.ds(i * NZF * ROWS + y, NZF, stride=ROWS), :].astype(BF)
-                out_v[4 * step + i, 2 * y] = value[:, 0:64]
-                out_v[4 * step + i, 2 * y + 1] = value[:, 64:128]
-        leave(step).start()
-        return carry
-
-    lax.fori_loop(0, 4, last, 0)
+                for dz, lanes in halves:
+                    acc[4 * step + 2 * i + dx, :, dz] += result[i * 128:(i + 1) * 128, lanes].reshape(8, ROWS, 128)
+        return carry
+
+    lax.fori_loop(0, 3, up_own, 0)
+    wait_rims(going, rim_dec, s_dec_rim)
+    going = start_rows(50, s_dec, s_dec_rim, y_dec, yr_dec)
+    lax.fori_loop(3, 4, up_own, 0)
+    n = NXM
+    for dst, first in ((up_dec, 9), (down_dec, 7)):
+        rows = slice(first, first + ROWS)
+        dst[0, 1:n + 1] = s_dec_rim[0:n, rows].astype(BF)
+        dst[1, 1:n + 1] = s_dec_rim[n:2 * n, rows].astype(BF)
+        dst[2] = s_dec_rim[2 * n:3 * n + 2, rows].astype(BF)
+        dst[3] = s_dec_rim[4 * n:5 * n + 2, rows].astype(BF)
+    sides = (rim_dec, up_dec, down_dec)
+    for low_high, x, first in ((0, 0, 0), (1, NXF - 1, 3)):
+        parts = [cells(ref, low_high, pl.ds(zt, 8)) for zt in range(3) for ref in sides]
+        result = dot(jnp.concatenate(parts, axis=1), w_rf_up[first].reshape(1152, 256))
+        for dz, lanes in halves:
+            acc[x, :, dz] += result[:, lanes].reshape(8, ROWS, 128)
+    acc_pairs = acc.reshape(8, 2, 8, 2, ROWS, 128)
+    for low_high, z, zt in ((2, 0, 0), (3, 7, 2)):
+        for dx in range(2):
+            parts = [cells(ref, low_high, pl.ds(xt + dx, 8)) for xt in range(2) for ref in sides]
+            result = dot(jnp.concatenate(parts, axis=1), w_rf_up[2 * dx:2 * dx + 2, zt].reshape(768, 256))
+            for dz, lanes in halves:
+                acc_pairs[:, dx, z, dz] += result[:, lanes].reshape(8, ROWS, 128)
+    wait_rows(going, s_dec_rim, yr_dec, y_dec_wide, y_dec_grid, y_dec_window, 1)
+    for number, row, slot in ((0, 0, 2), (1, ROWS - 1, 1)):
+        results = []
+        for dx in range(2):
+            parts = []
+            for xt in range(2):
+                for zt in range(3):
+                    parts.append(y_dec_window[number, zt, xt + dx:xt + dx + 8].reshape(64, 128).astype(BF))
+            part = dot(jnp.concatenate(parts, axis=1), w_rf_up[2 * dx:2 * dx + 2, :, slot].reshape(768, 256))
+            results.append(part.reshape(8, 8, 256))
+        result = jnp.stack(results, axis=1).reshape(128, 256)
+        for dz, lanes in halves:
+            acc_rows[pl.ds(dz * ROWS + row, 128, stride=32), :] += result[:, lanes]
+
+    def turn_out(x, carry):
+        for y in range(ROWS):
+            value = acc_rows[pl.ds(x * NZF * ROWS + y, NZF, stride=ROWS), :]
+            value = (value + bias_last).astype(BF)
+            out_v[x, 2 * y] = value[:, 0:64]
+            out_v[x, 2 * y + 1] = value[:, 64:128]
+        return carry
+
+    lax.fori_loop(0, NXF, turn_out, 0)
     for message_sent in sent:
         message_sent.wait_send()
-    for step in range(4):
-        leave(step).wait()
 
 
 def scratch():
     vmem = pltpu.VMEM
     fine = (NXF + 2, NZF + 2, ROWS, 128)
     mid = pool = (NXM + 2, NZM + 2, ROWS, 128)
+    rim = (4, NXF + 2, ROWS, 128)
+    rim_m = (4, NXM + 2, ROWS, 128)
     mid_s = (NXM + 4, NZM + 2, 32, 128)
     return [
-        vmem(fine, BF), vmem(fine, BF), vmem((NXF + 3, NZF + 2, 32, 128), F32), vmem((2, TF, 128), BF), vmem((2, TF, 128), BF),
-        vmem(fine, BF), vmem(fine, BF), vmem((2, TF, 128), BF), vmem((2, TF, 128), BF),
+        *[vmem(fine, BF), vmem(fine, BF), vmem(rim, BF), vmem(rim, BF), vmem((2, TF, 128), BF), vmem((2, TF, 128), BF)] * 2,
+        vmem((NXF, NZF, 32, 128), F32), vmem((96, 32, 128), F32), vmem((2, TF, 128), F32), vmem((2, NXF + 2, 32, 128), F32),
+        vmem((2, 4, NXF + 2, 8, 128), F32),
         vmem(pool, BF), vmem(pool, BF), vmem(mid_s, F32), vmem((2, TM, 128), BF), vmem((2, TM, 128), BF),
         vmem(mid, BF), vmem(mid, BF), vmem(mid, BF), vmem(mid_s, F32), vmem((2, TM, 128), BF), vmem((2, TM, 128), BF),
         vmem((8, 4, ROWS, 128), BF), vmem((8, 8, 32, 128), F32), vmem((2, 128, 128), BF), vmem((2, 128, 128), BF),
         vmem((256, 128), F32),
         vmem((8, 8, ROWS, 384), BF), vmem((2, 576, 128), F32), vmem((2, 36, 32, 128), F32), vmem((6, 6, ROWS, 768), BF),
-        vmem(mid, BF), vmem(mid, BF), vmem(mid, BF), vmem(mid_s, F32), vmem((2, TM, 128), BF), vmem((2, TM, 128), BF),
+        vmem(mid, BF), vmem(mid, BF), vmem(mid, BF), vmem(rim_m, BF), vmem(rim_m, BF), vmem(rim_m, BF),
+        vmem((2, TM, 128), BF), vmem((2, TM, 128), BF), vmem((NXM, NZM, 32, 128), F32), vmem((48, 32, 128), F32),
+        vmem((2, TM, 128), F32), vmem((2, NXM + 2, 32, 128), F32), vmem((2, 3, NXM + 2, 8, 128), F32),
         vmem((3, 3, 3, 64, 64), BF), vmem((3, 3, 3, 192, 64), BF), vmem((3, 3, 3, 256, 128), BF),
         vmem((3, 4, 4, 64, 256), BF), vmem((3, 4, 4, 64, 256), BF), vmem((3, 4, 4, 64, 256), BF),
         vmem((3, 3, 3, 128, 256), BF), vmem((3, 4, 3, 128, 256), BF), vmem((4, 3, 3, 256, 256), BF),
         vmem((4, 3, 3, 128, 256), BF),
-        vmem((NXF, 128, 256), F32), vmem((NXF, 32, NZF, 64), BF), vmem((NXF, 32, NZF, 64), BF),
-        vmem((4, 8, 2, ROWS, 128), F32),
+        vmem((NXF, 8, 2, ROWS, 128), F32), vmem((NXF, 32, NZF, 64), BF),
         pltpu.SemaphoreType.DMA((10 * LEVELS,)), pltpu.SemaphoreType.DMA((10 * LEVELS,)), pltpu.SemaphoreType.DMA((32,)),
     ]
 
@@ -494,12 +668,12 @@
     hbm = pl.BlockSpec(memory_space=pl.ANY)
     return pl.pallas_call(
         functools.partial(kernel, sizes),
-        out_shape=jax.ShapeDtypeStruct((NXF, 32, NZF, 64), BF),
+        out_shape=pltpu.VMEM((NXF, 32, NZF, 64), BF),
         in_specs=[hbm] * 6 + [pl.BlockSpec(memory_space=pltpu.VMEM)] * 5,
-        out_specs=hbm,
+        out_specs=pl.BlockSpec(memory_space=pltpu.VMEM),
         scratch_shapes=scratch(),
         compiler_params=pltpu.CompilerParams(
-            collective_id=0, has_side_effects=True, vmem_limit_bytes=62 * 2**20
+            collective_id=0, has_side_effects=True, vmem_limit_bytes=54 * 2**20
         ),
     )(volume, wf, wm, wb, wrm, wrf, *(bias.reshape(1, -1) for bias in (bf, bm, bb, brm, brf)))
 

time: 72.7 us -> 66.8 us (0.919); the launches traced: 72.6 us -> 65.5 us
  Pallas kernels: 66.8 us -> 61.7 us
  local copies, waits for them, and re-layouts: 5.78 us -> 3.74 us
    pallas_call x1, Pallas kernels: 66.8 us -> 61.7 us  [on_device(): pl.pallas_call(functools.partial(kernel, sizes), out_shape=pltpu.VMEM((NX...]
    unnamed x2, local copies, waits for them, and re-layouts: 5.78 us -> 3.74 us
where the time goes in v2:
time: 66.8 us; the launch traced here: 65.5 us
  Pallas kernels  61.7 us (92%)
  local copies, waits for them, and re-layouts  3.74 us (6%)
    pallas_call x1, Pallas kernels, on_device(): pl.pallas_call(functools.partial(kernel, sizes), out_shape=pltpu.VMEM((NX...  61.7 us
    unnamed x2, local copies, waits for them, and re-layouts  3.74 us

profile of v2, /device:TPU:2, one launch (start us, length us, event | category | flops | bytes accessed | tf_op | source)
XLA Modules:
  0.0 65.5 jit_solution(16296642562834901896)
XLA Ops:
  0.0 2.4 %copy.12.wrf_hbm = bf16[3,3,3,192,64]{4,3,2,1,0:T(8,128)(2,1)} copy(bf16[3,3,3,192,64]{3,4,2,1,0:T(8,128)(2,1)} %param.20) | data formatting | bytes 1327104 | tf_op args[9]
  2.4 61.7 %shard_map.109 = bf16[16,32,16,64]{3,2,1,0:T(8,128)(2,1)S(1)} custom-call(bf16[16,32,16,64]{3,2,1,0:T(8,128)(2,1)} %vol.1, bf16[3,3,3,64,64]{4,3,2,1,0:T(8,128)(2,1)} %wf_hbm.1, bf16[3,3,3,64,128]{4,3,2,1,0:T(8,128)(2,1)} %wm_hbm.1, bf16[3,3,3,128,256]{4,3,2,1,0:T(8,128)(2,1)} %wb_hbm.1, bf16[3,3,3,384,128]{4,3,2,1,0:T(8,128)(2,1)} %wrm_hbm.1, ...), custom_call_target="tpu_custom_call" | custom-call | tf_op jit(solution)/shard_map/pallas_call | solution.py:669
  64.2 1.3 %copy.14 = bf16[16,32,16,64]{3,2,1,0:T(8,128)(2,1)} copy(bf16[16,32,16,64]{3,2,1,0:T(8,128)(2,1)S(1)} %shard_map.109) | data formatting | bytes 2097152

commit v3 on v2

--- a/solution.py
+++ b/solution.py
@@ -39,7 +39,7 @@
     r_low, s_low, y_low, yr_low, pair_tmp,
     low_lanes, bottom_tmp, s_up, up_lanes,
     r_dec, hu_dec, hd_dec, rim_dec, up_dec, down_dec, y_dec, yr_dec, s_dec, s_dec_rim, y_dec_wide, y_dec_grid, y_dec_window,
-    wf_raw, wrf_raw, wrm_raw,
+    wf_raw, wrf_turned, wrf_raw, wrm_raw,
     w_fine, w_skip, w_mid, w_bottom, w_rm_skip, w_rm_up, w_rf_up,
     acc, vol_v,
     send_sem, recv_sem, local_sem,
@@ -83,19 +83,6 @@
         loads[name] = copy
 
     load("vol", vol, vol_v)
-    load("wf", wf_hbm, wf_raw)
-    load("wrf", wrf_hbm, wrf_raw)
-    for dz in range(2):
-        lanes = pl.ds(dz * 128, 128)
-        for q, slot in ((1, 0), (2, 2), (0, 3)):
-            load(("wm", dz, q), wm_hbm.at[:, q], w_mid.at[:, dz:dz + 3, slot, :, lanes])
-    for q, slot in ((1, 0), (2, 1), (0, 2)):
-        load(("wb", q), wb_hbm.at[:, q], w_bottom.at[:, :, slot])
-    for dz in range(2):
-        lanes = pl.ds(dz * 128, 128)
-        for q, slot in ((1, 0), (2, 1), (0, 2)):
-            load(("wrm", dz, q), wrm_hbm.at[:, q, :, 0:128, :], w_rm_skip.at[:, dz:dz + 3, slot, :, lanes])
-    load("wrm_raw", wrm_hbm.at[:, :, :, 128:384, :], wrm_raw)
 
     for ref in (r_in, h_in, r_enc, h_enc, r_dec, hu_dec, hd_dec):
         nx, nz = ref.shape[0], ref.shape[1]
@@ -114,7 +101,20 @@
     barrier = pltpu.get_barrier_semaphore()
     for peer in PEERS:
         pl.semaphore_signal(barrier, inc=1, device_id=near(peer), device_id_type=MESH)
-    pl.semaphore_wait(barrier, len(PEERS))
+
+    load("wf", wf_hbm, wf_raw)
+    load("wrf", wrf_hbm, wrf_turned)
+    for dz in range(2):
+        lanes = pl.ds(dz * 128, 128)
+        for q, slot in ((1, 0), (2, 2), (0, 3)):
+            load(("wm", dz, q), wm_hbm.at[:, q], w_mid.at[:, dz:dz + 3, slot, :, lanes])
+    for q, slot in ((1, 0), (2, 1), (0, 2)):
+        load(("wb", q), wb_hbm.at[:, q], w_bottom.at[:, :, slot])
+    for dz in range(2):
+        lanes = pl.ds(dz * 128, 128)
+        for q, slot in ((1, 0), (2, 1), (0, 2)):
+            load(("wrm", dz, q), wrm_hbm.at[:, q, :, 0:128, :], w_rm_skip.at[:, dz:dz + 3, slot, :, lanes])
+    load("wrm_raw", wrm_hbm.at[:, :, :, 128:384, :], wrm_raw)
 
     def start_xz(base, ref, depth):
         depths = depth if isinstance(depth, tuple) else (depth, depth)
@@ -205,15 +205,15 @@
         s[2 * n:3 * n + 2, 8:24] = rim[2].astype(F32)
         s[4 * n:5 * n + 2, 8:24] = rim[3].astype(F32)
 
-    def start_rows(base, s, s_side, ys, yr):
-        count, more = s.shape[0] * s.shape[1], s_side.shape[0]
-        rows, side_rows = s.reshape(count * 32, 128), s_side.reshape(more * 32, 128)
-        for number, row in enumerate((8, 23)):
-            ys[number, 0:count] = rows[pl.ds(row, count, stride=32), :].astype(BF)
-            ys[number, count:count + more] = side_rows[pl.ds(row, more, stride=32), :].astype(BF)
+    def start_rows(base, s, rows, ys, yr, first):
+        count = s.shape[0] if len(s.shape) == 3 else s.shape[0] * s.shape[1]
+        flat = s.reshape(count * 32, 128)
+        part = pl.ds(first, count)
+        for number, row in enumerate(rows):
+            ys[number, part] = flat[pl.ds(row, count, stride=32), :].astype(BF)
         return start([
-            message(base + 8, ys.at[0], yr.at[1], 0, -1, 0),
-            message(base + 9, ys.at[1], yr.at[0], 0, 1, 0),
+            message(base, ys.at[0, part], yr.at[1, part], 0, -1, 0),
+            message(base + 1, ys.at[1, part], yr.at[0, part], 0, 1, 0),
         ])
 
     def wait_rows(copies, s_side, yr, wide, grid, window, step):
@@ -351,13 +351,15 @@
         return carry
 
     lax.fori_loop(0, NXF, turn_in, 0)
+    pl.semaphore_wait(barrier, len(PEERS))
     going = start_rims(0, r_in, rim_in)
+    ends = start_rows(8, s_fine, (8, 23), y_in, yr_in, 0)
     fine_sides(s_fine, h_in)
     loads["wf"].wait()
     spread(wf_raw, 0, w_fine)
     fine_own(r_in, h_in, w_fine, 0, 6)
     wait_rims(going, rim_in, s_rim)
-    going = start_rows(0, s_fine, s_rim, y_in, yr_in)
+    ends += start_rows(10, s_rim, (8, 23), y_in, yr_in, 256)
     fine_own(r_in, h_in, w_fine, 6, 8)
     fine_rims(rim_in, side_in, w_fine)
     w_mid[:, :, 1] = jnp.zeros((3, 4, 64, 256), BF)
@@ -366,6 +368,20 @@
     w_rm_skip[:, 3, :, :, 0:128] = jnp.zeros((3, 3, 128, 128), BF)
     w_rm_skip[:, 0, :, :, 128:256] = jnp.zeros((3, 3, 128, 128), BF)
     loads["wrf"].wait()
+    same = lax.broadcasted_iota(jnp.int32, (192, 192), 0) == lax.broadcasted_iota(jnp.int32, (192, 192), 1)
+    identity = jnp.where(same, 1.0, 0.0).astype(BF)
+
+    def turn_weight(p, carry):
+        turned = lax.dot_general(
+            identity, wrf_turned[p].reshape(576, 192), (((1,), (1,)), ((), ())), preferred_element_type=F32
+        ).astype(BF)
+        for q in range(3):
+            for r in range(3):
+                first = (3 * q + r) * 64
+                wrf_raw[p, q, r] = turned[:, first:first + 64]
+        return carry
+
+    lax.fori_loop(0, 3, turn_weight, 0)
     spread(wrf_raw, 0, w_skip)
     loads["wrm_raw"].wait()
 
@@ -386,7 +402,7 @@
     w_rm_up[:, 2, :, :, 0:128] = jnp.zeros((4, 3, 256, 128), BF)
     lax.fori_loop(0, 16, rise_mid, 0)
 
-    wait_rows(going, s_rim, yr_in, y_wide, y_grid, y_window, 2)
+    wait_rows(ends, s_rim, yr_in, y_wide, y_grid, y_window, 2)
     fine_ends(w_fine)
 
     bias_fine = jnp.concatenate([bf_ref[...]] * 2, axis=1)
@@ -413,10 +429,9 @@
 
     lax.fori_loop(0, 8, fine, 0)
 
-    going = start_xz(10, r_pool, 1)
-    skipping = start_rims(20, r_enc, rim_enc)
+    going = start_xz(12, r_pool, 1)
     fine_sides(s_fine, h_enc)
-    fine_own(r_enc, h_enc, w_skip, 0, 4)
+    fine_own(r_enc, h_enc, w_skip, 0, 3)
 
     def rise_fine(chunk, carry):
         src = pl.ds(pl.multiple_of(64 + chunk * 16, 16), 16)
@@ -440,10 +455,10 @@
     lax.fori_loop(0, 8, rise_fine, 0)
 
     wait_xz(going, r_pool, s_pool)
-    going = start_y(10, s_pool, y_pool, yr_pool)
-    wait_rims(skipping, rim_enc, s_rim)
-    skipping = start_rows(20, s_fine, s_rim, y_enc, yr_enc)
-    fine_own(r_enc, h_enc, w_skip, 4, 5)
+    going = start_y(12, s_pool, y_pool, yr_pool)
+    skipping = start_rims(24, r_enc, rim_enc)
+    ends = start_rows(32, s_fine, (8, 23), y_enc, yr_enc, 0)
+    fine_own(r_enc, h_enc, w_skip, 3, 5)
     for dz in range(2):
         for q in range(3):
             loads[("wm", dz, q)].wait()
@@ -475,11 +490,12 @@
     low = jnp.maximum(pair_tmp[pl.ds(0, 128, stride=2), :], pair_tmp[pl.ds(1, 128, stride=2), :])
     r_low[2:6, 1:3] = low.astype(BF).reshape(4, 2, ROWS, 128)
 
-    going = start_xz(30, r_low, (2, 1))
-    middle = start_xz(40, r_mid, 1)
-
+    going = start_xz(36, r_low, (2, 1))
+    middle = start_xz(48, r_mid, 1)
+
+    wait_rims(skipping, rim_enc, s_rim)
+    ends += start_rows(34, s_rim, (8, 23), y_enc, yr_enc, 256)
     fine_own(r_enc, h_enc, w_skip, 5, 8)
-    fine_rims(rim_enc, side_enc, w_skip)
     arrived(going)
     clear_rim(r_low, (2, 1))
     low = r_low[...].astype(F32).reshape(8, 4, 2, 8, 128).reshape(8, 8, 8, 128)
@@ -490,14 +506,15 @@
     for number, row in enumerate((8, 9, 14, 15)):
         y_low[number // 2, pl.ds((number % 2) * 64, 64), :] = rows[pl.ds(row, 64, stride=32), :].astype(BF)
     going = start([
-        message(38, y_low.at[0], yr_low.at[1], 0, -1, 0),
-        message(39, y_low.at[1], yr_low.at[0], 0, 1, 0),
+        message(44, y_low.at[0], yr_low.at[1], 0, -1, 0),
+        message(45, y_low.at[1], yr_low.at[0], 0, 1, 0),
     ])
     wait_xz(middle, r_mid, s_mid)
-    middle = start_y(40, s_mid, y_mid, yr_mid)
+    middle = start_y(48, s_mid, y_mid, yr_mid)
+    fine_rims(rim_enc, side_enc, w_skip)
     for q in range(3):
         loads[("wb", q)].wait()
-    wait_rows(skipping, s_rim, yr_enc, y_wide, y_grid, y_window, 2)
+    wait_rows(ends, s_rim, yr_enc, y_wide, y_grid, y_window, 2)
     fine_ends(w_skip)
     arrived(going)
     for number, row in enumerate((6, 7, 16, 17)):
@@ -561,7 +578,8 @@
             r_dec_pairs[place + index] = value.astype(BF)
             s_dec_pairs[:, dx, :, dz, 8:24] = value
 
-    going = start_rims(50, r_dec, rim_dec)
+    going = start_rims(60, r_dec, rim_dec)
+    ends = start_rows(68, s_dec, (8, 23), y_dec, yr_dec, 0)
 
     def dec_sides(x, carry):
         hu_dec[x + 1, 1:NZM + 1] = s_dec[x, :, 9:25].astype(BF)
@@ -587,7 +605,7 @@
 
     lax.fori_loop(0, 3, up_own, 0)
     wait_rims(going, rim_dec, s_dec_rim)
-    going = start_rows(50, s_dec, s_dec_rim, y_dec, yr_dec)
+    ends += start_rows(70, s_dec_rim, (8, 23), y_dec, yr_dec, 64)
     lax.fori_loop(3, 4, up_own, 0)
     n = NXM
     for dst, first in ((up_dec, 9), (down_dec, 7)):
@@ -609,7 +627,7 @@
             result = dot(jnp.concatenate(parts, axis=1), w_rf_up[2 * dx:2 * dx + 2, zt].reshape(768, 256))
             for dz, lanes in halves:
                 acc_pairs[:, dx, z, dz] += result[:, lanes].reshape(8, ROWS, 128)
-    wait_rows(going, s_dec_rim, yr_dec, y_dec_wide, y_dec_grid, y_dec_window, 1)
+    wait_rows(ends, s_dec_rim, yr_dec, y_dec_wide, y_dec_grid, y_dec_window, 1)
     for number, row, slot in ((0, 0, 2), (1, ROWS - 1, 1)):
         results = []
         for dx in range(2):
@@ -655,12 +673,12 @@
         vmem(mid, BF), vmem(mid, BF), vmem(mid, BF), vmem(rim_m, BF), vmem(rim_m, BF), vmem(rim_m, BF),
         vmem((2, TM, 128), BF), vmem((2, TM, 128), BF), vmem((NXM, NZM, 32, 128), F32), vmem((48, 32, 128), F32),
         vmem((2, TM, 128), F32), vmem((2, NXM + 2, 32, 128), F32), vmem((2, 3, NXM + 2, 8, 128), F32),
-        vmem((3, 3, 3, 64, 64), BF), vmem((3, 3, 3, 192, 64), BF), vmem((3, 3, 3, 256, 128), BF),
+        vmem((3, 3, 3, 64, 64), BF), vmem((3, 3, 3, 64, 192), BF), vmem((3, 3, 3, 192, 64), BF), vmem((3, 3, 3, 256, 128), BF),
         vmem((3, 4, 4, 64, 256), BF), vmem((3, 4, 4, 64, 256), BF), vmem((3, 4, 4, 64, 256), BF),
         vmem((3, 3, 3, 128, 256), BF), vmem((3, 4, 3, 128, 256), BF), vmem((4, 3, 3, 256, 256), BF),
         vmem((4, 3, 3, 128, 256), BF),
         vmem((NXF, 8, 2, ROWS, 128), F32), vmem((NXF, 32, NZF, 64), BF),
-        pltpu.SemaphoreType.DMA((10 * LEVELS,)), pltpu.SemaphoreType.DMA((10 * LEVELS,)), pltpu.SemaphoreType.DMA((32,)),
+        pltpu.SemaphoreType.DMA((12 * LEVELS,)), pltpu.SemaphoreType.DMA((12 * LEVELS,)), pltpu.SemaphoreType.DMA((32,)),
     ]
 
 
@@ -673,9 +691,9 @@
         out_specs=pl.BlockSpec(memory_space=pltpu.VMEM),
         scratch_shapes=scratch(),
         compiler_params=pltpu.CompilerParams(
-            collective_id=0, has_side_effects=True, vmem_limit_bytes=54 * 2**20
+            collective_id=0, has_side_effects=True, vmem_limit_bytes=56 * 2**20
         ),
-    )(volume, wf, wm, wb, wrm, wrf, *(bias.reshape(1, -1) for bias in (bf, bm, bb, brm, brf)))
+    )(volume, wf, wm, wb, wrm, wrf.transpose(0, 1, 2, 4, 3), *(bias.reshape(1, -1) for bias in (bf, bm, bb, brm, brf)))
 
 
 def solution(mesh):

time: 66.8 us -> 60.4 us (0.904)
  Pallas kernels: 61.7 us -> 58.4 us
  local copies, waits for them, and re-layouts: 3.74 us -> 1.32 us
    pallas_call x1, Pallas kernels: 61.7 us -> 58.4 us  [on_device(): pl.pallas_call(functools.partial(kernel, sizes), out_shape=pltpu.VMEM((NX...]
    unnamed x2 -> x1, local copies, waits for them, and re-layouts: 3.74 us -> 1.32 us
where the time goes in v3:
time: 60.4 us; the launch traced here: 59.7 us
  Pallas kernels  58.4 us (97%)
  local copies, waits for them, and re-layouts  1.32 us (2%)
    pallas_call x1, Pallas kernels, on_device(): pl.pallas_call(functools.partial(kernel, sizes), out_shape=pltpu.VMEM((NX...  58.4 us
    unnamed x1, local copies, waits for them, and re-layouts  1.32 us

profile of v3, /device:TPU:2, one launch (start us, length us, event | category | flops | bytes accessed | tf_op | source)
XLA Modules:
  0.0 59.7 jit_solution(10902201768344858774)
XLA Ops:
  0.0 58.4 %shard_map.109 = bf16[16,32,16,64]{3,2,1,0:T(8,128)(2,1)S(1)} custom-call(bf16[16,32,16,64]{3,2,1,0:T(8,128)(2,1)} %vol.1, bf16[3,3,3,64,64]{4,3,2,1,0:T(8,128)(2,1)} %wf_hbm.1, bf16[3,3,3,64,128]{4,3,2,1,0:T(8,128)(2,1)} %wm_hbm.1, bf16[3,3,3,128,256]{4,3,2,1,0:T(8,128)(2,1)} %wb_hbm.1, bf16[3,3,3,384,128]{4,3,2,1,0:T(8,128)(2,1)} %wrm_hbm.1, ...), custom_call_target="tpu_custom_call" | custom-call | tf_op jit(solution)/shard_map/pallas_call | solution.py:687
  58.4 1.3 %copy.13 = bf16[16,32,16,64]{3,2,1,0:T(8,128)(2,1)} copy(bf16[16,32,16,64]{3,2,1,0:T(8,128)(2,1)S(1)} %shard_map.109) | data formatting | bytes 2097152

commit v4 on v3

--- a/solution.py
+++ b/solution.py
@@ -82,7 +82,26 @@
         copy.start()
         loads[name] = copy
 
-    load("vol", vol, vol_v)
+    for name, planes in (("vol_low", pl.ds(0, 1)), ("vol_high", pl.ds(NXF - 1, 1)), ("vol", pl.ds(1, NXF - 2))):
+        load(name, vol.at[planes], vol_v.at[planes])
+
+    barrier = pltpu.get_barrier_semaphore()
+    for peer in PEERS:
+        pl.semaphore_signal(barrier, inc=1, device_id=near(peer), device_id_type=MESH)
+
+    load("wf", wf_hbm, wf_raw)
+    load("wrf", wrf_hbm, wrf_turned)
+    for dz in range(2):
+        lanes = pl.ds(dz * 128, 128)
+        for q, slot in ((1, 0), (2, 2), (0, 3)):
+            load(("wm", dz, q), wm_hbm.at[:, q], w_mid.at[:, dz:dz + 3, slot, :, lanes])
+    for q, slot in ((1, 0), (2, 1), (0, 2)):
+        load(("wb", q), wb_hbm.at[:, q], w_bottom.at[:, :, slot])
+    for dz in range(2):
+        lanes = pl.ds(dz * 128, 128)
+        for q, slot in ((1, 0), (2, 1), (0, 2)):
+            load(("wrm", dz, q), wrm_hbm.at[:, q, :, 0:128, :], w_rm_skip.at[:, dz:dz + 3, slot, :, lanes])
+    load("wrm_raw", wrm_hbm.at[:, :, :, 128:384, :], wrm_raw)
 
     for ref in (r_in, h_in, r_enc, h_enc, r_dec, hu_dec, hd_dec):
         nx, nz = ref.shape[0], ref.shape[1]
@@ -98,25 +117,7 @@
         for row in (7, 24):
             rows[pl.ds(row, count, stride=32), :] = jnp.zeros((count, 128), F32)
 
-    barrier = pltpu.get_barrier_semaphore()
-    for peer in PEERS:
-        pl.semaphore_signal(barrier, inc=1, device_id=near(peer), device_id_type=MESH)
-
-    load("wf", wf_hbm, wf_raw)
-    load("wrf", wrf_hbm, wrf_turned)
-    for dz in range(2):
-        lanes = pl.ds(dz * 128, 128)
-        for q, slot in ((1, 0), (2, 2), (0, 3)):
-            load(("wm", dz, q), wm_hbm.at[:, q], w_mid.at[:, dz:dz + 3, slot, :, lanes])
-    for q, slot in ((1, 0), (2, 1), (0, 2)):
-        load(("wb", q), wb_hbm.at[:, q], w_bottom.at[:, :, slot])
-    for dz in range(2):
-        lanes = pl.ds(dz * 128, 128)
-        for q, slot in ((1, 0), (2, 1), (0, 2)):
-            load(("wrm", dz, q), wrm_hbm.at[:, q, :, 0:128, :], w_rm_skip.at[:, dz:dz + 3, slot, :, lanes])
-    load("wrm_raw", wrm_hbm.at[:, :, :, 128:384, :], wrm_raw)
-
-    def start_xz(base, ref, depth):
+    def start_xz(base, ref, depth, first=0, last=8):
         depths = depth if isinstance(depth, tuple) else (depth, depth)
         nx, nz = ref.shape[0] - 2 * depths[0], ref.shape[1] - 2 * depths[1]
 
@@ -131,7 +132,8 @@
         copies = []
         for number, (dx, dz) in enumerate(((-1, -1), (-1, 1), (1, -1), (1, 1), (-1, 0), (1, 0), (0, -1), (0, 1))):
             (src_x, dst_x), (src_z, dst_z) = part(nx, dx, depths[0]), part(nz, dz, depths[1])
-            copies.append(message(base + number, ref.at[src_x, src_z], ref.at[dst_x, dst_z], dx, 0, dz))
+            if first <= number < last:
+                copies.append(message(base + number, ref.at[src_x, src_z], ref.at[dst_x, dst_z], dx, 0, dz))
         return start(copies)
 
     def clear_rim(ref, depth):
@@ -173,19 +175,20 @@
         rows[pl.ds(7, count, stride=32), :] = low
         rows[pl.ds(24, count, stride=32), :] = high
 
-    def start_rims(base, ref, rim):
+    def start_rims(base, ref, rim, first=0, last=8):
         nx, nz = ref.shape[0] - 2, ref.shape[1] - 2
         own_x, own_z = pl.ds(1, nx), pl.ds(1, nz)
-        return start([
-            message(base, ref.at[1, 1], rim.at[3, nx + 1], -1, 0, -1),
-            message(base + 1, ref.at[1, nz], rim.at[2, nx + 1], -1, 0, 1),
-            message(base + 2, ref.at[nx, 1], rim.at[3, 0], 1, 0, -1),
-            message(base + 3, ref.at[nx, nz], rim.at[2, 0], 1, 0, 1),
-            message(base + 4, ref.at[1, own_z], rim.at[1, own_z], -1, 0, 0),
-            message(base + 5, ref.at[nx, own_z], rim.at[0, own_z], 1, 0, 0),
-            message(base + 6, ref.at[own_x, 1], rim.at[3, own_x], 0, 0, -1),
-            message(base + 7, ref.at[own_x, nz], rim.at[2, own_x], 0, 0, 1),
-        ])
+        paths = (
+            (ref.at[1, 1], rim.at[3, nx + 1], -1, 0, -1),
+            (ref.at[1, nz], rim.at[2, nx + 1], -1, 0, 1),
+            (ref.at[nx, 1], rim.at[3, 0], 1, 0, -1),
+            (ref.at[nx, nz], rim.at[2, 0], 1, 0, 1),
+            (ref.at[1, own_z], rim.at[1, own_z], -1, 0, 0),
+            (ref.at[nx, own_z], rim.at[0, own_z], 1, 0, 0),
+            (ref.at[own_x, 1], rim.at[3, own_x], 0, 0, -1),
+            (ref.at[own_x, nz], rim.at[2, own_x], 0, 0, 1),
+        )
+        return start([message(base + number, *paths[number]) for number in range(first, last)])
 
     def wait_rims(copies, rim, s):
         arrived(copies)
@@ -340,7 +343,6 @@
             for dz, lanes in halves:
                 acc_rows[pl.ds(dz * ROWS + row, 128, stride=32), :] += result[:, lanes]
 
-    loads["vol"].wait()
     fine_rows = s_fine.reshape(NXF * NZF * 32, 128)
 
     def turn_in(x, carry):
@@ -350,9 +352,14 @@
         r_in[x + 1, 1:NZF + 1] = s_fine[x, :, 8:24].astype(BF)
         return carry
 
-    lax.fori_loop(0, NXF, turn_in, 0)
+    loads["vol_low"].wait()
+    loads["vol_high"].wait()
+    lax.fori_loop(0, 2, lambda i, carry: turn_in(i * (NXF - 1), carry), 0)
     pl.semaphore_wait(barrier, len(PEERS))
-    going = start_rims(0, r_in, rim_in)
+    going = start_rims(0, r_in, rim_in, 0, 6)
+    loads["vol"].wait()
+    lax.fori_loop(1, NXF - 1, turn_in, 0)
+    going += start_rims(0, r_in, rim_in, 6, 8)
     ends = start_rows(8, s_fine, (8, 23), y_in, yr_in, 0)
     fine_sides(s_fine, h_in)
     loads["wf"].wait()
@@ -367,41 +374,6 @@
     w_mid[:, 0, :, :, 128:256] = jnp.zeros((3, 4, 64, 128), BF)
     w_rm_skip[:, 3, :, :, 0:128] = jnp.zeros((3, 3, 128, 128), BF)
     w_rm_skip[:, 0, :, :, 128:256] = jnp.zeros((3, 3, 128, 128), BF)
-    loads["wrf"].wait()
-    same = lax.broadcasted_iota(jnp.int32, (192, 192), 0) == lax.broadcasted_iota(jnp.int32, (192, 192), 1)
-    identity = jnp.where(same, 1.0, 0.0).astype(BF)
-
-    def turn_weight(p, carry):
-        turned = lax.dot_general(
-            identity, wrf_turned[p].reshape(576, 192), (((1,), (1,)), ((), ())), preferred_element_type=F32
-        ).astype(BF)
-        for q in range(3):
-            for r in range(3):
-                first = (3 * q + r) * 64
-                wrf_raw[p, q, r] = turned[:, first:first + 64]
-        return carry
-
-    lax.fori_loop(0, 3, turn_weight, 0)
-    spread(wrf_raw, 0, w_skip)
-    loads["wrm_raw"].wait()
-
-    def sums(parts):
-        return (parts[0], parts[1] + parts[2], parts[0] + parts[1], parts[2])
-
-    def rise_mid(chunk, carry):
-        rows = pl.ds(pl.multiple_of(chunk * 16, 16), 16)
-        for q, slot in ((1, 0), (2, 1), (0, 2)):
-            by_r = [sums([wrm_raw[p, q, r, rows, :].astype(F32) for p in range(3)]) for r in range(3)]
-            for x_sum in range(4):
-                z_sums = sums([by_r[r][x_sum] for r in range(3)])
-                for z_sum, (zt, dz) in enumerate(((0, 0), (1, 0), (1, 1), (2, 1))):
-                    w_rm_up[x_sum, zt, slot, rows, dz * 128:(dz + 1) * 128] = z_sums[z_sum].astype(BF)
-        return carry
-
-    w_rm_up[:, 0, :, :, 128:256] = jnp.zeros((4, 3, 256, 128), BF)
-    w_rm_up[:, 2, :, :, 0:128] = jnp.zeros((4, 3, 256, 128), BF)
-    lax.fori_loop(0, 16, rise_mid, 0)
-
     wait_rows(ends, s_rim, yr_in, y_wide, y_grid, y_window, 2)
     fine_ends(w_fine)
 
@@ -427,12 +399,53 @@
             s_pool_pairs[(pair + 1,) + index + (pl.ds(8, 16),)] = most[:, half]
         return carry
 
-    lax.fori_loop(0, 8, fine, 0)
-
-    going = start_xz(12, r_pool, 1)
+    lax.fori_loop(0, 2, lambda i, carry: fine(i * 7, carry), 0)
+    going = start_xz(12, r_pool, 1, 0, 6)
+    lax.fori_loop(1, 7, fine, 0)
+
+    going += start_xz(12, r_pool, 1, 6, 8)
+    loads["wrf"].wait()
+    same = lax.broadcasted_iota(jnp.int32, (192, 192), 0) == lax.broadcasted_iota(jnp.int32, (192, 192), 1)
+    identity = jnp.where(same, 1.0, 0.0).astype(BF)
+
+    def turn_weight(p, carry):
+        turned = lax.dot_general(
+            identity, wrf_turned[p].reshape(576, 192), (((1,), (1,)), ((), ())), preferred_element_type=F32
+        ).astype(BF)
+        for q in range(3):
+            for r in range(3):
+                first = (3 * q + r) * 64
+                wrf_raw[p, q, r] = turned[:, first:first + 64]
+        return carry
+
+    lax.fori_loop(0, 3, turn_weight, 0)
+    spread(wrf_raw, 0, w_skip)
     fine_sides(s_fine, h_enc)
-    fine_own(r_enc, h_enc, w_skip, 0, 3)
-
+    fine_own(r_enc, h_enc, w_skip, 0, 2)
+    loads["wrm_raw"].wait()
+
+    def sums(parts):
+        return (parts[0], parts[1] + parts[2], parts[0] + parts[1], parts[2])
+
+    def rise_mid(chunk, carry):
+        rows = pl.ds(pl.multiple_of(chunk * 16, 16), 16)
+        for q, slot in ((1, 0), (2, 1), (0, 2)):
+            by_r = [sums([wrm_raw[p, q, r, rows, :].astype(F32) for p in range(3)]) for r in range(3)]
+            for x_sum in range(4):
+                z_sums = sums([by_r[r][x_sum] for r in range(3)])
+                for z_sum, (zt, dz) in enumerate(((0, 0), (1, 0), (1, 1), (2, 1))):
+                    w_rm_up[x_sum, zt, slot, rows, dz * 128:(dz + 1) * 128] = z_sums[z_sum].astype(BF)
+        return carry
+
+    w_rm_up[:, 0, :, :, 128:256] = jnp.zeros((4, 3, 256, 128), BF)
+    w_rm_up[:, 2, :, :, 0:128] = jnp.zeros((4, 3, 256, 128), BF)
+    lax.fori_loop(0, 16, rise_mid, 0)
+
+
+    wait_xz(going, r_pool, s_pool)
+    going = start_y(12, s_pool, y_pool, yr_pool)
+    skipping = start_rims(24, r_enc, rim_enc)
+    ends = start_rows(32, s_fine, (8, 23), y_enc, yr_enc, 0)
     def rise_fine(chunk, carry):
         src = pl.ds(pl.multiple_of(64 + chunk * 16, 16), 16)
         rows = pl.ds(pl.multiple_of(chunk * 16, 16), 16)
@@ -454,11 +467,7 @@
     w_rf_up[:, 2, :, :, 0:128] = jnp.zeros((4, 3, 128, 128), BF)
     lax.fori_loop(0, 8, rise_fine, 0)
 
-    wait_xz(going, r_pool, s_pool)
-    going = start_y(12, s_pool, y_pool, yr_pool)
-    skipping = start_rims(24, r_enc, rim_enc)
-    ends = start_rows(32, s_fine, (8, 23), y_enc, yr_enc, 0)
-    fine_own(r_enc, h_enc, w_skip, 3, 5)
+    fine_own(r_enc, h_enc, w_skip, 2, 4)
     for dz in range(2):
         for q in range(3):
             loads[("wm", dz, q)].wait()
@@ -495,7 +504,7 @@
 
     wait_rims(skipping, rim_enc, s_rim)
     ends += start_rows(34, s_rim, (8, 23), y_enc, yr_enc, 256)
-    fine_own(r_enc, h_enc, w_skip, 5, 8)
+    fine_own(r_enc, h_enc, w_skip, 4, 8)
     arrived(going)
     clear_rim(r_low, (2, 1))
     low = r_low[...].astype(F32).reshape(8, 4, 2, 8, 128).reshape(8, 8, 8, 128)
@@ -511,11 +520,8 @@
     ])
     wait_xz(middle, r_mid, s_mid)
     middle = start_y(48, s_mid, y_mid, yr_mid)
-    fine_rims(rim_enc, side_enc, w_skip)
     for q in range(3):
         loads[("wb", q)].wait()
-    wait_rows(ends, s_rim, yr_enc, y_wide, y_grid, y_window, 2)
-    fine_ends(w_skip)
     arrived(going)
     for number, row in enumerate((6, 7, 16, 17)):
         edge = at_low("gy") if number < 2 else at_high("gy")
@@ -579,6 +585,7 @@
             s_dec_pairs[:, dx, :, dz, 8:24] = value
 
     going = start_rims(60, r_dec, rim_dec)
+    ends_enc = ends
     ends = start_rows(68, s_dec, (8, 23), y_dec, yr_dec, 0)
 
     def dec_sides(x, carry):
@@ -603,10 +610,13 @@
                     acc[4 * step + 2 * i + dx, :, dz] += result[i * 128:(i + 1) * 128, lanes].reshape(8, ROWS, 128)
         return carry
 
-    lax.fori_loop(0, 3, up_own, 0)
+    lax.fori_loop(0, 2, up_own, 0)
+    fine_rims(rim_enc, side_enc, w_skip)
+    wait_rows(ends_enc, s_rim, yr_enc, y_wide, y_grid, y_window, 2)
+    fine_ends(w_skip)
     wait_rims(going, rim_dec, s_dec_rim)
     ends += start_rows(70, s_dec_rim, (8, 23), y_dec, yr_dec, 64)
-    lax.fori_loop(3, 4, up_own, 0)
+    lax.fori_loop(2, 4, up_own, 0)
     n = NXM
     for dst, first in ((up_dec, 9), (down_dec, 7)):
         rows = slice(first, first + ROWS)

time: 60.4 us -> 57.7 us (0.955)
  Pallas kernels: 58.4 us -> 55.8 us
    pallas_call x1, Pallas kernels: 58.4 us -> 55.8 us  [on_device(): pl.pallas_call(functools.partial(kernel, sizes), out_shape=pltpu.VMEM((NX...]
where the time goes in v4:
time: 57.7 us; the launch traced here: 57.1 us
  Pallas kernels  55.8 us (97%)
  local copies, waits for them, and re-layouts  1.32 us (2%)
    pallas_call x1, Pallas kernels, on_device(): pl.pallas_call(functools.partial(kernel, sizes), out_shape=pltpu.VMEM((NX...  55.8 us
    unnamed x1, local copies, waits for them, and re-layouts  1.32 us

profile of v4, /device:TPU:2, one launch (start us, length us, event | category | flops | bytes accessed | tf_op | source)
XLA Modules:
  0.0 57.1 jit_solution(3942931732401289543)
XLA Ops:
  0.0 55.8 %shard_map.109 = bf16[16,32,16,64]{3,2,1,0:T(8,128)(2,1)S(1)} custom-call(bf16[16,32,16,64]{3,2,1,0:T(8,128)(2,1)} %vol.1, bf16[3,3,3,64,64]{4,3,2,1,0:T(8,128)(2,1)} %wf_hbm.1, bf16[3,3,3,64,128]{4,3,2,1,0:T(8,128)(2,1)} %wm_hbm.1, bf16[3,3,3,128,256]{4,3,2,1,0:T(8,128)(2,1)} %wb_hbm.1, bf16[3,3,3,384,128]{4,3,2,1,0:T(8,128)(2,1)} %wrm_hbm.1, ...), custom_call_target="tpu_custom_call" | custom-call | tf_op jit(solution)/shard_map/pallas_call | solution.py:697
  55.8 1.3 %copy.13 = bf16[16,32,16,64]{3,2,1,0:T(8,128)(2,1)} copy(bf16[16,32,16,64]{3,2,1,0:T(8,128)(2,1)S(1)} %shard_map.109) | data formatting | bytes 2097152

commit v5 on v4

--- a/solution.py
+++ b/solution.py
@@ -467,7 +467,7 @@
     w_rf_up[:, 2, :, :, 0:128] = jnp.zeros((4, 3, 128, 128), BF)
     lax.fori_loop(0, 8, rise_fine, 0)
 
-    fine_own(r_enc, h_enc, w_skip, 2, 4)
+    fine_own(r_enc, h_enc, w_skip, 2, 3)
     for dz in range(2):
         for q in range(3):
             loads[("wm", dz, q)].wait()
@@ -504,7 +504,7 @@
 
     wait_rims(skipping, rim_enc, s_rim)
     ends += start_rows(34, s_rim, (8, 23), y_enc, yr_enc, 256)
-    fine_own(r_enc, h_enc, w_skip, 4, 8)
+    fine_own(r_enc, h_enc, w_skip, 3, 8)
     arrived(going)
     clear_rim(r_low, (2, 1))
     low = r_low[...].astype(F32).reshape(8, 4, 2, 8, 128).reshape(8, 8, 8, 128)

time: 57.7 us -> 58.1 us (level)
  no operation moved by 1% of the time
where the time goes in v5:
time: 58.1 us; the launch traced here: 57.5 us
  Pallas kernels  56.2 us (97%)
  local copies, waits for them, and re-layouts  1.32 us (2%)
    pallas_call x1, Pallas kernels, on_device(): pl.pallas_call(functools.partial(kernel, sizes), out_shape=pltpu.VMEM((NX...  56.2 us
    unnamed x1, local copies, waits for them, and re-layouts  1.32 us

profile of v5, /device:TPU:2, one launch (start us, length us, event | category | flops | bytes accessed | tf_op | source)
XLA Modules:
  0.0 57.5 jit_solution(8513432937571018895)
XLA Ops:
  0.0 56.2 %shard_map.109 = bf16[16,32,16,64]{3,2,1,0:T(8,128)(2,1)S(1)} custom-call(bf16[16,32,16,64]{3,2,1,0:T(8,128)(2,1)} %vol.1, bf16[3,3,3,64,64]{4,3,2,1,0:T(8,128)(2,1)} %wf_hbm.1, bf16[3,3,3,64,128]{4,3,2,1,0:T(8,128)(2,1)} %wm_hbm.1, bf16[3,3,3,128,256]{4,3,2,1,0:T(8,128)(2,1)} %wb_hbm.1, bf16[3,3,3,384,128]{4,3,2,1,0:T(8,128)(2,1)} %wrm_hbm.1, ...), custom_call_target="tpu_custom_call" | custom-call | tf_op jit(solution)/shard_map/pallas_call | solution.py:697
  56.2 1.3 %copy.13 = bf16[16,32,16,64]{3,2,1,0:T(8,128)(2,1)} copy(bf16[16,32,16,64]{3,2,1,0:T(8,128)(2,1)S(1)} %shard_map.109) | data formatting | bytes 2097152
